TPU v7x, 32 devices: a whole 2x2x4 slice. The times are simulated.
32 devices in a mesh: grp: 2 (over y), tm: 8 (over z, x), apa: 2 (over core).
Axes of the slice: x: 2, y: 2, z: 4, core: 2. Of those that a mesh axis runs over, the one named last changes fastest.
Arguments:
- waveforms: bfloat16 [5120, 2048], P(('grp', 'apa'), 'tm'), parts along dimension 0, may hold values from -6 to 6
- time_kernel: bfloat16 [3, 64], replicated, may hold values from -0.75 to 0.75
- wire_slot: int32 [5120], P('grp'), parts along dimension 0, may hold values from 0 to 2559, each once
- tick_offset: int32 [5120], P('grp'), parts along dimension 0, may hold values from 0 to 63
- bad_channel: int32 [5120], P('grp'), parts along dimension 0, may hold values 0 or 1
- induction_real: float32 [2, 800], replicated, may hold values from 0.5 to 2
- induction_imaginary: float32 [2, 800], replicated, may hold values from -1 to 1
- induction_filter: float32 [2, 800], replicated, may hold values from 0.2 to 1
- collection_real: float32 [960], replicated, may hold values from 0.5 to 2
- collection_imaginary: float32 [960], replicated, may hold values from -1 to 1
- collection_filter: float32 [960], replicated, may hold values from 0.2 to 1
Outputs:
- deconvolved: float32 [5120, 2048], P('grp', ('tm', 'apa')), parts along dimension 0
There are 2 independent parts, one for each index of `grp`. A program takes and returns all parts, laid end to end along the dimension named above; an argument that names none is the same for every part. Nothing has to cross between parts.
Inputs may be any that keep to these rules, and one draw needn't show every extreme that they name: A permutation: readout channel c is slot wire_slot[c] of the plane layout, whose assemblies hold 2560 slots each, U wires first, then V, then W. `bad_channel`: 1 marks a bad channel.
All inputs are finite; a program needn't handle non-finite values.
Results may differ from a plain program's by a relative error of at most 0.0051.
Values may be sent and summed in bfloat16 or wider, within the bound.
A program may use at most 64 MiB of HBM per device.

v0:
```python
import math

import jax
import jax.numpy as jnp
from jax import lax
from jax.sharding import PartitionSpec as P

INDUCTION_WIRES = 800
COLLECTION_WIRES = 960
OFFSET_RANGE = 64


def shifted(value, axis, steps):
    count = lax.axis_size(axis)
    pairs = [(source, (source + steps) % count) for source in range(count)]
    return lax.ppermute(value, axis, pairs)


def slot_plane(slot_index):
    assembly_wires = 2 * INDUCTION_WIRES + COLLECTION_WIRES
    within = slot_index % assembly_wires
    return (within >= INDUCTION_WIRES).astype(jnp.int32) + (within >= 2 * INDUCTION_WIRES).astype(
        jnp.int32
    )


def fourier_tables(wire_count):
    positions = jnp.arange(wire_count, dtype=jnp.int32)
    phase_turns = positions[:, None] * positions[None, :] % wire_count
    phase_angle = phase_turns.astype(jnp.float32) * (2.0 * math.pi / wire_count)
    cosine = jnp.cos(phase_angle).astype(jnp.bfloat16)
    sine_table = jnp.sin(phase_angle).astype(jnp.bfloat16)
    forward = jnp.concatenate([cosine, sine_table], 0)
    backward = jnp.concatenate([cosine, -sine_table], 1)
    return (forward, backward)


def wire_deconvolve(plane_rows, tables, response_real, response_imaginary, filter_gain):
    forward, backward = tables
    wire_count = plane_rows.shape[0]
    magnitude = response_real * response_real + response_imaginary * response_imaginary
    ratio_real = (filter_gain * response_real / magnitude)[:, None]
    ratio_imaginary = (-filter_gain * response_imaginary / magnitude)[:, None]
    spectrum = jnp.dot(forward, plane_rows, preferred_element_type=jnp.float32)
    cosine_part = spectrum[:wire_count]
    sine_part = spectrum[wire_count:]
    product = jnp.concatenate(
        [
            cosine_part * ratio_real + sine_part * ratio_imaginary,
            cosine_part * ratio_imaginary - sine_part * ratio_real,
        ],
        0,
    ).astype(jnp.bfloat16)
    return jnp.dot(backward, product, preferred_element_type=jnp.float32) * (1.0 / wire_count)


def deconvolve_planes(
    ordered,
    induction_real,
    induction_imaginary,
    induction_filter,
    collection_real,
    collection_imaginary,
    collection_filter,
):
    induction_tables = fourier_tables(INDUCTION_WIRES)
    collection_tables = fourier_tables(COLLECTION_WIRES)
    results = []
    for plane_index in range(2):
        row_start = plane_index * INDUCTION_WIRES
        results.append(
            wire_deconvolve(
                ordered[row_start : row_start + INDUCTION_WIRES],
                induction_tables,
                induction_real[plane_index],
                induction_imaginary[plane_index],
                induction_filter[plane_index],
            )
        )
    row_start = 2 * INDUCTION_WIRES
    results.append(
        wire_deconvolve(
            ordered[row_start : row_start + COLLECTION_WIRES],
            collection_tables,
            collection_real,
            collection_imaginary,
            collection_filter,
        )
    )
    return jnp.concatenate(results, 0)


def toeplitz(kernel_row):
    tap_count = kernel_row.shape[0]
    padded = jnp.concatenate(
        [
            jnp.zeros((tap_count - 1,), kernel_row.dtype),
            kernel_row,
            jnp.zeros((tap_count,), kernel_row.dtype),
        ]
    )
    padded_length = padded.shape[0]
    rolled = jnp.roll(padded, 1 - 2 * tap_count)
    tiled = jnp.tile(rolled, 2 * tap_count)[: 2 * tap_count * (padded_length - 1)]
    return tiled.reshape(2 * tap_count, padded_length - 1)[:, :tap_count]


def shift_rows(extended, offsets, length):
    current = extended
    for bit_number in range((OFFSET_RANGE - 1).bit_length()):
        step_ticks = 1 << bit_number
        moved = jnp.concatenate(
            [jnp.zeros((current.shape[0], step_ticks), current.dtype), current[:, :-step_ticks]], 1
        )
        chosen = offsets >> bit_number & 1 == 1
        current = jnp.where(chosen[:, None], moved, current)
    return current[:, OFFSET_RANGE : OFFSET_RANGE + length]


def convolve(aligned, table, tap_count):
    row_count = aligned.shape[0]
    blocks = aligned.reshape(row_count, aligned.shape[1] // tap_count, tap_count)
    result = jnp.einsum(
        "cjq,qr->cjr", blocks[:, :-1], table[:tap_count], preferred_element_type=jnp.float32
    )
    result = result + jnp.einsum(
        "cjq,qr->cjr", blocks[:, 1:], table[tap_count:], preferred_element_type=jnp.float32
    )
    return result.reshape(row_count, -1)


def local(
    waveforms,
    time_kernel,
    wire_slot,
    tick_offset,
    bad_channel,
    induction_real,
    induction_imaginary,
    induction_filter,
    collection_real,
    collection_imaginary,
    collection_filter,
):
    tap_count = time_kernel.shape[1]
    tail_ticks = tap_count + OFFSET_RANGE
    channel_count = wire_slot.shape[0]
    inverse = (
        jnp.zeros((channel_count,), jnp.int32)
        .at[wire_slot]
        .set(jnp.arange(channel_count, dtype=jnp.int32))
    )
    tables = [toeplitz(time_kernel[plane_index]) for plane_index in range(3)]
    row_count = waveforms.shape[0]
    first_row = lax.axis_index("apa") * row_count
    local_offset = lax.dynamic_slice_in_dim(tick_offset, first_row, row_count)
    local_bad = lax.dynamic_slice_in_dim(bad_channel, first_row, row_count)
    local_plane = slot_plane(lax.dynamic_slice_in_dim(wire_slot, first_row, row_count))
    masked = waveforms * (1 - local_bad).astype(jnp.bfloat16)[:, None]
    earlier = shifted(masked[:, -tail_ticks:], "tm", 1)
    aligned = shift_rows(
        jnp.concatenate([earlier, masked], 1), local_offset, masked.shape[1] + tap_count
    )
    summed = jnp.zeros(masked.shape, jnp.float32)
    for plane_index in range(3):
        summed = summed + jnp.where(
            (local_plane == plane_index)[:, None],
            convolve(aligned, tables[plane_index], tap_count),
            0.0,
        )
    filtered = summed.astype(jnp.bfloat16)
    regrouped = lax.all_to_all(filtered, "apa", split_axis=1, concat_axis=0, tiled=True)
    ordered = regrouped[inverse]
    return deconvolve_planes(
        ordered,
        induction_real,
        induction_imaginary,
        induction_filter,
        collection_real,
        collection_imaginary,
        collection_filter,
    )


def solution(mesh):
    placed = (
        P(("grp", "apa"), "tm"),
        P(),
        P("grp"),
        P("grp"),
        P("grp"),
        P(),
        P(),
        P(),
        P(),
        P(),
        P(),
    )
    return jax.shard_map(
        local, mesh=mesh, in_specs=placed, out_specs=P("grp", ("tm", "apa")), check_vma=False
    )
```

profile of v0, /device:TPU:0, one launch (start us, length us, event | category | flops | bytes accessed | tf_op | source)
XLA Modules:
  0.0 106.4 jit_solution(6117354309688895531)
XLA Ops:
  0.0 0.8 subtract_convert_fusion.3
  0.8 1.3 %broadcast_multiply_fusion = bf16[1280,256]{1,0:T(8,128)(2,1)S(1)} fusion(bf16[1280,256]{1,0:T(8,128)(2,1)} %param.11, bf16[1280]{0:T(1024)(128)(2,1)S(1)} %subtract_convert_fusion.3), kind=kLoop, calls=%fused_computation.83 | loop fusion | flops 327680 | bytes 1313280 | tf_op jit(solution)/shard_map/mul | solution.py:159
  2.2 3.0 %collective-permute-start = (bf16[1280,128]{1,0:T(8,128)(2,1)S(1)}, bf16[1280,128]{1,0:T(8,128)(2,1)S(1)}, u32[]{:S(2)}, u32[]{:S(2)}) collective-permute-start(bf16[1280,128]{1,0:T(8,128)(2,1)S(1)} %slice.176), channel_id=1, source_target_pairs={{0,2},{2,4},{4,6},{6,8},{8,10},{10,12},{12,14},{14,0},{1,3},{3,5},... | collective-permute-start | bytes 983048 | tf_op jit(solution)/shard_map/ppermute | solution.py:16
  5.3 12.9 %sine_convert_fusion.1 = (bf16[800,800]{1,0:T(8,128)(2,1)}, bf16[800,800]{1,0:T(8,128)(2,1)S(1)}) fusion(), kind=kLoop, calls=%fused_computation.23 | loop fusion | flops 7040000 | bytes 2560000 | tf_op jit(solution)/shard_map/convert_element_type | solution.py:32
  18.2 11.9 %fusion.33 = bf16[800,800]{1,0:T(8,128)(2,1)} fusion(), kind=kLoop, calls=%fused_computation.58 | loop fusion | flops 8320000 | bytes 1280000 | tf_op jit(solution)/shard_map/neg | solution.py:34
  30.1 16.1 %fusion.32 = bf16[960,960]{1,0:T(8,128)(2,1)} fusion(), kind=kLoop, calls=%fused_computation.57 | loop fusion | flops 11980800 | bytes 1843200 | tf_op jit(solution)/shard_map/neg | solution.py:34
  46.3 10.1 %scatter_custom_fusion = s32[2560]{0:T(1024)S(1)} fusion(s32[2560]{0:T(1024)S(1)} %compare_select_fusion.1, s32[2560]{0:T(1024)S(1)} %iota.17, s32[]{:T(128)} %constant.20.clone.1), kind=kCustom, calls=%fused_computation.109 | custom fusion | bytes 10244 | tf_op jit(solution)/shard_map/scatter | solution.py:151
  56.5 0.6 fusion.62
  59.1 17.3 %sine_convert_fusion = (bf16[960,960]{1,0:T(8,128)(2,1)}, bf16[960,960]{1,0:T(8,128)(2,1)}) fusion(), kind=kLoop, calls=%fused_computation.10 | loop fusion | flops 10137600 | bytes 3686400 | tf_op jit(solution)/shard_map/convert_element_type | solution.py:32
  76.5 0.9 fusion.31
  77.5 0.9 pad_select_fusion.3
  78.4 0.9 pad_select_fusion.2
  79.3 0.9 pad_select_fusion.1
  80.2 0.9 pad_select_fusion
  81.2 1.0 slice_select_fusion
  82.1 0.6 copy.14
  82.7 0.4 fusion.37
  83.1 0.4 convolution_add_fusion.2
  83.4 0.4 fusion.39
  83.8 0.3 convolution_add_fusion.1
  84.5 0.4 convolution_add_fusion
  85.1 4.3 %all_to_all.16 = bf16[1280,2,128]{0,2,1:T(8,128)(2,1)S(1)} all-to-all(bf16[1280,2,128]{0,2,1:T(8,128)(2,1)S(1)} %fusion.23), channel_id=1, replica_groups=mesh['grp'=2,'tm'=8,'apa'=2] {'apa'}, dimensions={1} | all-to-all | bytes 1310720 | tf_op jit(solution)/shard_map/all_to_all | solution.py:172
  89.7 6.1 %gather_fusion = bf16[2560,128]{1,0:T(8,128)(2,1)} fusion(bf16[2560,128]{1,0:T(8,128)(2,1)S(1)} %bitcast.60, s32[3072]{0:T(1024)S(1)} %pad_clamp_fusion), kind=kCustom, calls=%fused_computation | custom fusion | bytes 1320960 | tf_op jit(solution)/shard_map/gather | solution.py:173
  95.9 1.9 %fusion.19 = f32[1600,128]{1,0:T(8,128)S(1)} fusion(bf16[800,800]{1,0:T(8,128)(2,1)S(1)} %copy-done.4, bf16[800,800]{1,0:T(8,128)(2,1)S(1)} %get-tuple-element.34, bf16[2560,128]{1,0:T(8,128)(2,1)} %gather_fusion), kind=kOutput, calls=%fused_computation.34 | convolution fusion | flops 332800000 | bytes 3584000 | tf_op jit(solution)/shard_map/dot_general | solution.py:44
  97.8 0.9 fusion.18
  99.2 0.9 fusion.28
  100.4 0.9 fusion.29
  101.3 0.6 copy-done.1
  101.9 0.6 copy-done.2
  102.5 1.2 %fusion.2 = f32[1920,128]{1,0:T(8,128)S(1)} fusion(bf16[960,960]{1,0:T(8,128)(2,1)S(1)} %copy-done.2, bf16[960,960]{1,0:T(8,128)(2,1)S(1)} %copy-done.1, bf16[2560,128]{1,0:T(8,128)(2,1)S(1)} %copy-done.5), kind=kOutput, calls=%fused_computation.6 | convolution fusion | flops 479232000 | bytes 5160960 | tf_op jit(solution)/shard_map/dot_general | solution.py:44
  104.0 1.2 %fusion.25 = f32[960,128]{1,0:T(8,128)S(1)} fusion(bf16[960,960]{1,0:T(8,128)(2,1)S(1)} %copy-done, bf16[960,960]{1,0:T(8,128)(2,1)S(1)} %copy-done.1, bf16[960,128]{1,0:T(8,128)(2,1)S(1)} %get-tuple-element.13, bf16[960,128]{1,0:T(8,128)(2,1)S(1)} %get-tuple-element.12), kind=kOutput, calls=%fused_computation.44 | convolution fusion | flops 480337920 | bytes 4669440 | tf_op jit(solution)/shard_map/dot_general | solution.py:54
  105.2 1.1 %pad_maximum_fusion.6 = f32[2560,128]{1,0:T(8,128)} fusion(f32[960,128]{1,0:T(8,128)S(1)} %fusion.25, f32[800,128]{1,0:T(8,128)S(1)} %fusion.29, f32[800,128]{1,0:T(8,128)S(1)} %fusion.28), kind=kLoop, calls=%fused_computation.37 | loop fusion | flops 655360 | bytes 2621440 | tf_op jit(solution)/shard_map/concatenate | solution.py:90
  (60 shorter events, 4.3 us)
Async XLA Ops:
  0.0 5.1 %copy-start.6 = (s32[2560]{0:T(1024)S(1)}, s32[2560]{0:T(1024)}, u32[]{:S(2)}) copy-start(s32[2560]{0:T(1024)} %param.13) | copy-start | bytes 30724
  2.2 74.2 %collective-permute-start = (bf16[1280,128]{1,0:T(8,128)(2,1)S(1)}, bf16[1280,128]{1,0:T(8,128)(2,1)S(1)}, u32[]{:S(2)}, u32[]{:S(2)}) collective-permute-start(bf16[1280,128]{1,0:T(8,128)(2,1)S(1)} %slice.176), channel_id=1, source_target_pairs={{0,2},{2,4},{4,6},{6,8},{8,10},{10,12},{12,14},{14,0},{1,3},{3,5},... | collective-permute-start | bytes 983048 | tf_op jit(solution)/shard_map/ppermute | solution.py:16
  18.1 28.1 %copy-start.11 = (s32[2560]{0:T(1024)S(1)}, s32[2560]{0:T(1024)}, u32[]{:S(2)}) copy-start(s32[2560]{0:T(1024)} %param.14) | copy-start | bytes 30724
  18.1 28.2 %copy-start.15 = (bf16[3,64]{1,0:T(4,128)(2,1)S(1)}, bf16[3,64]{1,0:T(4,128)(2,1)}, u32[]{:S(2)}) copy-start(bf16[3,64]{1,0:T(4,128)(2,1)} %param.12) | copy-start | bytes 1156
  18.1 38.4 %copy-start.8 = (f32[2,800]{1,0:T(2,128)S(1)}, f32[2,800]{1,0:T(2,128)}, u32[]{:S(2)}) copy-start(f32[2,800]{1,0:T(2,128)} %param.16) | copy-start | bytes 19204
  18.1 38.4 %copy-start.9 = (f32[2,800]{1,0:T(2,128)S(1)}, f32[2,800]{1,0:T(2,128)}, u32[]{:S(2)}) copy-start(f32[2,800]{1,0:T(2,128)} %param.18) | copy-start | bytes 19204
  18.1 38.4 %copy-start.10 = (f32[2,800]{1,0:T(2,128)S(1)}, f32[2,800]{1,0:T(2,128)}, u32[]{:S(2)}) copy-start(f32[2,800]{1,0:T(2,128)} %param.17) | copy-start | bytes 19204
  18.1 39.0 %copy-start.12 = (f32[960]{0:T(1024)S(1)}, f32[960]{0:T(1024)}, u32[]{:S(2)}) copy-start(f32[960]{0:T(1024)} %param.21) | copy-start | bytes 11524
  18.2 39.0 %copy-start.13 = (f32[960]{0:T(1024)S(1)}, f32[960]{0:T(1024)}, u32[]{:S(2)}) copy-start(f32[960]{0:T(1024)} %param.19) | copy-start | bytes 11524
  18.2 39.0 %copy-start.14 = (f32[960]{0:T(1024)S(1)}, f32[960]{0:T(1024)}, u32[]{:S(2)}) copy-start(f32[960]{0:T(1024)} %param.20) | copy-start | bytes 11524
  89.7 6.1 %copy-start.4 = (bf16[800,800]{1,0:T(8,128)(2,1)S(1)}, bf16[800,800]{1,0:T(8,128)(2,1)}, u32[]{:S(2)}) copy-start(bf16[800,800]{1,0:T(8,128)(2,1)} %get-tuple-element.33) | copy-start | bytes 3840004
  95.9 1.9 %copy-start.5 = (bf16[2560,128]{1,0:T(8,128)(2,1)S(1)}, bf16[2560,128]{1,0:T(8,128)(2,1)}, u32[]{:S(2)}) copy-start(bf16[2560,128]{1,0:T(8,128)(2,1)} %gather_fusion) | copy-start | bytes 1966084
  97.8 0.9 copy-start.7
  97.8 1.4 %copy-start.3 = (bf16[800,800]{1,0:T(8,128)(2,1)S(1)}, bf16[800,800]{1,0:T(8,128)(2,1)}, u32[]{:S(2)}) copy-start(bf16[800,800]{1,0:T(8,128)(2,1)} %fusion.33) | copy-start | bytes 3840004
  100.4 1.5 %copy-start.1 = (bf16[960,960]{1,0:T(8,128)(2,1)S(1)}, bf16[960,960]{1,0:T(8,128)(2,1)}, u32[]{:S(2)}) copy-start(bf16[960,960]{1,0:T(8,128)(2,1)} %get-tuple-element.32) | copy-start | bytes 5529604
  100.4 2.1 %copy-start.2 = (bf16[960,960]{1,0:T(8,128)(2,1)S(1)}, bf16[960,960]{1,0:T(8,128)(2,1)}, u32[]{:S(2)}) copy-start(bf16[960,960]{1,0:T(8,128)(2,1)} %get-tuple-element.31) | copy-start | bytes 5529604
  102.5 1.5 %copy-start = (bf16[960,960]{1,0:T(8,128)(2,1)S(1)}, bf16[960,960]{1,0:T(8,128)(2,1)}, u32[]{:S(2)}) copy-start(bf16[960,960]{1,0:T(8,128)(2,1)} %fusion.32) | copy-start | bytes 5529604
where the time goes:
time: 107 us; the launch traced here: 106 us
  other arithmetic  69.1 us (65%)
  local copies, waits for them, and re-layouts  20.5 us (19%)
  matrix products  9.13 us (9%)
  blocking collectives  4.26 us (4%)
  starting transfers between devices  2.99 us (3%)
    convert_element_type x2, other arithmetic, fourier_tables(): sine_table = jnp.sin(phase_angle).astype(jnp.bfloat16)  30.1 us
    neg x2, other arithmetic, fourier_tables(): backward = jnp.concatenate([cosine, -sine_table], 1)  28 us
    scatter x1, local copies, waits for them, and re-layouts, local(): inverse = jnp.zeros((channel_count,), jnp.int32).at[wire_slot].set(jnp.ar...  10.1 us
    gather x1, local copies, waits for them, and re-layouts, local(): ordered = regrouped[inverse]  6.13 us
    select_n x6, other arithmetic, shift_rows(): current = jnp.where(chosen[:, None], moved, current)  5.58 us
    all_to_all x1, blocking collectives, local(): lax.all_to_all(filtered, 'apa', split_axis=1, concat_axis=0, tiled=True)  4.26 us
    dot_general x3, matrix products, wire_deconvolve(): spectrum = jnp.dot(forward, plane_rows, preferred_element_type=jnp.float32)  4.03 us
    dot_general x3, matrix products, wire_deconvolve(): jnp.dot(backward, product, preferred_element_type=jnp.float32)  2.99 us
  transfers between devices with their start and end apart: 1, of which 0 were waited for; matrix products, arithmetic and copies ran while one was open for 67% of the time, Pallas kernels for 0%

commit v1 on v0

--- a/solution.py
+++ b/solution.py
@@ -2,6 +2,8 @@
 
 import jax
 import jax.numpy as jnp
+import ml_dtypes
+import numpy as np
 from jax import lax
 from jax.sharding import PartitionSpec as P
 
@@ -25,13 +27,13 @@
 
 
 def fourier_tables(wire_count):
-    positions = jnp.arange(wire_count, dtype=jnp.int32)
+    positions = np.arange(wire_count, dtype=np.int64)
     phase_turns = positions[:, None] * positions[None, :] % wire_count
-    phase_angle = phase_turns.astype(jnp.float32) * (2.0 * math.pi / wire_count)
-    cosine = jnp.cos(phase_angle).astype(jnp.bfloat16)
-    sine_table = jnp.sin(phase_angle).astype(jnp.bfloat16)
-    forward = jnp.concatenate([cosine, sine_table], 0)
-    backward = jnp.concatenate([cosine, -sine_table], 1)
+    phase_angle = phase_turns * (2.0 * math.pi / wire_count)
+    cosine = np.cos(phase_angle).astype(ml_dtypes.bfloat16)
+    sine_table = np.sin(phase_angle).astype(ml_dtypes.bfloat16)
+    forward = np.concatenate([cosine, sine_table], 0)
+    backward = np.concatenate([cosine, -sine_table], 1)
     return (forward, backward)
 
 

time: 107 us -> 50.3 us (0.47)
  other arithmetic: 69.1 us -> 10.2 us
  matrix products: 9.13 us -> 10.7 us
    convert_element_type x2 -> x0, other arithmetic: 30.1 us -> none  [fourier_tables(): sine_table = jnp.sin(phase_angle).astype(jnp.bfloat16)]
    neg x2 -> x0, other arithmetic: 28 us -> none  [fourier_tables(): backward = jnp.concatenate([cosine, -sine_table], 1)]
    dot_general x3 -> x6, matrix products: 2.99 us -> 4.53 us  [wire_deconvolve(): jnp.dot(backward, product, preferred_element_type=jnp.float32)]
    unnamed x32 -> x34, local copies, waits for them, and re-layouts: 1.44 us -> 2.53 us
  transfers between devices with their start and end apart: 1 -> 1, of which waited for: 0 -> 0; matrix products, arithmetic and copies ran while one was open for 67% -> 25% of each run, Pallas kernels for 0% -> 0%
where the time goes in v1:
time: 50.3 us; the launch traced here: 49.9 us
  local copies, waits for them, and re-layouts  21.4 us (43%)
  matrix products  10.7 us (21%)
  other arithmetic  10.2 us (20%)
  blocking collectives  4.26 us (8%)
  starting transfers between devices  2.99 us (6%)
    scatter x1, local copies, waits for them, and re-layouts, local(): inverse = jnp.zeros((channel_count,), jnp.int32).at[wire_slot].set(jnp.ar...  9.93 us
    gather x1, local copies, waits for them, and re-layouts, local(): ordered = regrouped[inverse]  6.14 us
    select_n x6, other arithmetic, shift_rows(): current = jnp.where(chosen[:, None], moved, current)  5.6 us
    dot_general x6, matrix products, wire_deconvolve(): jnp.dot(backward, product, preferred_element_type=jnp.float32)  4.53 us
    all_to_all x1, blocking collectives, local(): lax.all_to_all(filtered, 'apa', split_axis=1, concat_axis=0, tiled=True)  4.26 us
    dot_general x3, matrix products, wire_deconvolve(): spectrum = jnp.dot(forward, plane_rows, preferred_element_type=jnp.float32)  4.03 us
    ppermute x1, starting transfers between devices, shifted(): return lax.ppermute(value, axis, pairs)  2.99 us
    unnamed x34, local copies, waits for them, and re-layouts  2.53 us
  transfers between devices with their start and end apart: 1, of which 0 were waited for; matrix products, arithmetic and copies ran while one was open for 25% of the time, Pallas kernels for 0%

profile of v1, /device:TPU:0, one launch (start us, length us, event | category | flops | bytes accessed | tf_op | source)
XLA Modules:
  0.0 49.9 jit_solution(7467742581757089391)
XLA Ops:
  0.0 0.8 %subtract_convert_fusion.6 = bf16[1280]{0:T(1024)(128)(2,1)S(1)} fusion(s32[2560]{0:T(1024)} %param.19, s32[]{:T(128)S(6)} %select_n.50), kind=kLoop, calls=%fused_computation.72 | loop fusion | flops 2560 | bytes 7684 | tf_op jit(solution)/shard_map/convert_element_type | solution.py:161
  0.9 1.4 %broadcast_multiply_fusion = bf16[1280,256]{1,0:T(8,128)(2,1)S(1)} fusion(bf16[1280,256]{1,0:T(8,128)(2,1)} %param.15, bf16[1280]{0:T(1024)(128)(2,1)S(1)} %subtract_convert_fusion.6), kind=kLoop, calls=%fused_computation.46 | loop fusion | flops 327680 | bytes 1313280 | tf_op jit(solution)/shard_map/mul | solution.py:161
  2.3 3.0 %collective-permute-start = (bf16[1280,128]{1,0:T(8,128)(2,1)S(1)}, bf16[1280,128]{1,0:T(8,128)(2,1)S(1)}, u32[]{:S(2)}, u32[]{:S(2)}) collective-permute-start(bf16[1280,128]{1,0:T(8,128)(2,1)S(1)} %slice.182), channel_id=1, source_target_pairs={{0,2},{2,4},{4,6},{6,8},{8,10},{10,12},{12,14},{14,0},{1,3},{3,5},... | collective-permute-start | bytes 983048 | tf_op jit(solution)/shard_map/ppermute | solution.py:18
  7.4 9.9 %scatter_custom_fusion = s32[2560]{0:T(1024)S(1)} fusion(s32[2560]{0:T(1024)S(1)} %compare_select_fusion.1, s32[2560]{0:T(1024)S(1)} %iota.3, s32[]{:T(128)} %constant.21.clone.1), kind=kCustom, calls=%fused_computation.84 | custom fusion | bytes 10244 | tf_op jit(solution)/shard_map/scatter | solution.py:153
  17.4 0.6 %fusion.42 = (f32[800]{0:T(1024)S(1)}, f32[800]{0:T(1024)}, f32[800]{0:T(1024)S(1)}, f32[800]{0:T(1024)S(1)}) fusion(f32[2,800]{1,0:T(2,128)S(1)} %copy-done.9, f32[2,800]{1,0:T(2,128)S(1)} %copy-done.10, f32[2,800]{1,0:T(2,128)S(1)} %copy-done.11), kind=kLoop, calls=%fused_computation.97 | loop fusion | flops 12800 | bytes 32000 | tf_op jit(solution)/shard_map/div | solution.py:44
  18.2 1.0 %fusion.10 = bf16[1280,384]{1,0:T(8,128)(2,1)S(1)} fusion(bf16[1280,256]{1,0:T(8,128)(2,1)S(1)} %broadcast_multiply_fusion, bf16[1280,128]{1,0:T(8,128)(2,1)S(1)} %collective-permute-done, bf16[1280,383]{1,0:T(8,128)(2,1)S(1)} %fusion.9, pred[1280]{0:T(1024)(128)(4,1)S(1)} %get-tuple-element.19), kind=kLoop, calls=%fused_computation.25 | loop fusion | flops 2457600 | bytes 2947840 | tf_op jit(solution)/shard_map/jit(_where)/select_n | solution.py:118
  19.2 0.9 %pad_select_fusion.3 = bf16[1280,384]{1,0:T(8,128)(2,1)S(1)} fusion(bf16[1280,384]{1,0:T(8,128)(2,1)S(1)} %fusion.10, bf16[1280,382]{1,0:T(8,128)(2,1)S(1)} %bitcast.82, pred[1280]{0:T(1024)(128)(4,1)S(1)} %get-tuple-element.18), kind=kLoop, calls=%fused_computation.30 | loop fusion | flops 491520 | bytes 2945280 | tf_op jit(solution)/shard_map/jit(_where)/select_n | solution.py:118
  20.1 0.9 %pad_select_fusion.2 = bf16[1280,384]{1,0:T(8,128)(2,1)S(1)} fusion(bf16[1280,384]{1,0:T(8,128)(2,1)S(1)} %pad_select_fusion.3, bf16[1280,380]{1,0:T(8,128)(2,1)S(1)} %bitcast.84, pred[1280]{0:T(1024)(128)(4,1)S(1)} %get-tuple-element.17), kind=kLoop, calls=%fused_computation.29 | loop fusion | flops 491520 | bytes 2940160 | tf_op jit(solution)/shard_map/jit(_where)/select_n | solution.py:118
  21.1 0.9 %pad_select_fusion.1 = bf16[1280,384]{1,0:T(8,128)(2,1)S(1)} fusion(bf16[1280,384]{1,0:T(8,128)(2,1)S(1)} %pad_select_fusion.2, bf16[1280,376]{1,0:T(8,128)(2,1)S(1)} %bitcast.85, pred[1280]{0:T(1024)(128)(4,1)S(1)} %get-tuple-element.16), kind=kLoop, calls=%fused_computation.28 | loop fusion | flops 491520 | bytes 2929920 | tf_op jit(solution)/shard_map/jit(_where)/select_n | solution.py:118
  22.0 0.9 %pad_select_fusion = bf16[1280,384]{1,0:T(8,128)(2,1)S(1)} fusion(bf16[1280,384]{1,0:T(8,128)(2,1)S(1)} %pad_select_fusion.1, bf16[1280,368]{1,0:T(8,128)(2,1)S(1)} %bitcast.86, pred[1280]{0:T(1024)(128)(4,1)S(1)} %get-tuple-element.15), kind=kLoop, calls=%fused_computation.27 | loop fusion | flops 491520 | bytes 2909440 | tf_op jit(solution)/shard_map/jit(_where)/select_n | solution.py:118
  22.9 1.0 %slice_select_fusion = bf16[1280,320]{1,0:T(8,128)(2,1)S(1)} fusion(bf16[1280,384]{1,0:T(8,128)(2,1)S(1)} %pad_select_fusion, bf16[1280,352]{1,0:T(8,128)(2,1)S(1)} %bitcast.83, pred[1280]{0:T(1024)(128)(4,1)S(1)} %get-tuple-element.14), kind=kLoop, calls=%fused_computation.26 | loop fusion | flops 409600 | bytes 2540800 | tf_op jit(solution)/shard_map/jit(_where)/select_n | solution.py:118
  23.9 0.6 %copy.18 = bf16[1280,320]{0,1:T(8,128)(2,1)S(1)} copy(bf16[1280,320]{1,0:T(8,128)(2,1)S(1)} %slice_select_fusion) | data formatting | bytes 1638400 | tf_op jit(solution)/shard_map/slice | solution.py:119
  24.5 0.4 fusion.14
  24.8 0.3 convolution_add_fusion.2
  25.6 0.4 convolution_add_fusion.1
  25.9 0.4 fusion.18
  26.3 0.3 convolution_add_fusion
  26.9 4.3 %all_to_all.16 = bf16[1280,2,128]{0,2,1:T(8,128)(2,1)S(1)} all-to-all(bf16[1280,2,128]{0,2,1:T(8,128)(2,1)S(1)} %fusion.1), channel_id=1, replica_groups=mesh['grp'=2,'tm'=8,'apa'=2] {'apa'}, dimensions={1} | all-to-all | bytes 1310720 | tf_op jit(solution)/shard_map/all_to_all | solution.py:174
  31.5 6.1 %gather_fusion = bf16[2560,128]{1,0:T(8,128)(2,1)} fusion(bf16[2560,128]{1,0:T(8,128)(2,1)S(1)} %bitcast.75, s32[3072]{0:T(1024)S(1)} %pad_clamp_fusion), kind=kCustom, calls=%fused_computation | custom fusion | bytes 1320960 | tf_op jit(solution)/shard_map/gather | solution.py:175
  37.6 1.9 %fusion.31 = f32[1600,128]{1,0:T(8,128)S(1)} fusion(bf16[1600,800]{1,0:T(8,128)(2,1)S(1)} %copy-done, bf16[2560,128]{1,0:T(8,128)(2,1)} %gather_fusion), kind=kOutput, calls=%fused_computation.58 | convolution fusion | flops 327680000 | bytes 3584000 | tf_op jit(solution)/shard_map/dot_general | solution.py:46
  39.6 0.9 %fusion.29 = f32[1600,128]{1,0:T(8,128)S(1)} fusion(bf16[1600,800]{1,0:T(8,128)(2,1)S(1)} %copy-done, bf16[2560,128]{1,0:T(8,128)(2,1)S(1)} %copy-done.4), kind=kOutput, calls=%fused_computation.56 | convolution fusion | flops 327680000 | bytes 3891200 | tf_op jit(solution)/shard_map/dot_general | solution.py:46
  40.5 0.4 copy-done.2
  40.9 0.7 %fusion.33 = f32[128,800]{0,1:T(8,128)S(1)} fusion(bf16[800,800]{1,0:T(8,128)(2,1)S(1)} %copy-done.2, f32[1600,128]{1,0:T(8,128)S(1)} %fusion.31, f32[800]{0:T(1024)S(1)} %copy-done.7, f32[800]{0:T(1024)S(1)} %get-tuple-element.5), kind=kOutput, calls=%fused_computation.60 | convolution fusion | flops 164249600 | bytes 2515200 | tf_op jit(solution)/shard_map/dot_general | solution.py:56
  42.0 0.7 %fusion.8 = f32[800,128]{1,0:T(8,128)S(1)} fusion(f32[128,800]{0,1:T(8,128)S(1)} %fusion.33, bf16[800,800]{1,0:T(8,128)(2,1)S(1)} %copy-done.3, f32[1600,128]{1,0:T(8,128)S(1)} %fusion.31, f32[800]{0:T(1024)S(1)} %copy-done.7, f32[800]{0:T(1024)S(1)} %get-tuple-element.5), kind=kOutput, calls=%fused_computation.20 | convolution fusion | flops 164454400 | bytes 2924800 | tf_op jit(solution)/shard_map/dot_general | solution.py:56
  42.7 0.7 %fusion.34 = f32[128,800]{0,1:T(8,128)S(1)} fusion(bf16[800,800]{1,0:T(8,128)(2,1)S(1)} %copy-done.2, f32[1600,128]{1,0:T(8,128)S(1)} %fusion.29, f32[800]{0:T(1024)S(1)} %get-tuple-element.7, f32[800]{0:T(1024)S(1)} %get-tuple-element.8), kind=kOutput, calls=%fused_computation.61 | convolution fusion | flops 164249600 | bytes 2515200 | tf_op jit(solution)/shard_map/dot_general | solution.py:56
  43.4 0.7 %fusion.6 = f32[800,128]{1,0:T(8,128)S(1)} fusion(f32[128,800]{0,1:T(8,128)S(1)} %fusion.34, bf16[800,800]{1,0:T(8,128)(2,1)S(1)} %copy-done.3, f32[1600,128]{1,0:T(8,128)S(1)} %fusion.29, f32[800]{0:T(1024)S(1)} %get-tuple-element.7, f32[800]{0:T(1024)S(1)} %get-tuple-element.8), kind=kOutput, calls=%fused_computation.17 | convolution fusion | flops 164454400 | bytes 2924800 | tf_op jit(solution)/shard_map/dot_general | solution.py:56
  44.1 0.7 %copy-done.1 = bf16[1920,960]{1,0:T(8,128)(2,1)S(1)} copy-done((bf16[1920,960]{1,0:T(8,128)(2,1)S(1)}, bf16[1920,960]{1,0:T(8,128)(2,1)}, u32[]{:S(2)}) %copy-start.1) | copy-done | bytes 3686424
  44.8 1.2 %fusion.22 = f32[1920,128]{1,0:T(8,128)S(1)} fusion(bf16[1920,960]{1,0:T(8,128)(2,1)S(1)} %copy-done.1, bf16[2560,128]{1,0:T(8,128)(2,1)S(1)} %copy-done.4), kind=kOutput, calls=%fused_computation.49 | convolution fusion | flops 471859200 | bytes 5160960 | tf_op jit(solution)/shard_map/dot_general | solution.py:46
  46.4 0.8 %fusion.24 = f32[128,960]{0,1:T(8,128)S(1)} fusion(bf16[960,960]{1,0:T(8,128)(2,1)S(1)} %copy-done.6, f32[1920,128]{1,0:T(8,128)S(1)} %fusion.22, f32[960]{0:T(1024)S(1)} %get-tuple-element.13, f32[960]{0:T(1024)S(1)} %get-tuple-element.12), kind=kOutput, calls=%fused_computation.51 | convolution fusion | flops 236421120 | bytes 3325440 | tf_op jit(solution)/shard_map/dot_general | solution.py:56
  47.2 0.7 %copy-done.5 = bf16[960,960]{1,0:T(8,128)(2,1)S(1)} copy-done((bf16[960,960]{1,0:T(8,128)(2,1)S(1)}, bf16[960,960]{1,0:T(8,128)(2,1)}, u32[]{:S(2)}) %copy-start.5) | copy-done | bytes 1843224
  47.9 0.9 %fusion.4 = f32[960,128]{1,0:T(8,128)S(1)} fusion(f32[128,960]{0,1:T(8,128)S(1)} %fusion.24, bf16[960,960]{1,0:T(8,128)(2,1)S(1)} %copy-done.5, f32[1920,128]{1,0:T(8,128)S(1)} %fusion.22, f32[960]{0:T(1024)S(1)} %get-tuple-element.13, f32[960]{0:T(1024)S(1)} %get-tuple-element.12), kind=kOutput, calls=%fused_computation.14 | convolution fusion | flops 236666880 | bytes 3816960 | tf_op jit(solution)/shard_map/dot_general | solution.py:56
  48.8 1.1 %pad_maximum_fusion = f32[2560,128]{1,0:T(8,128)} fusion(f32[960,128]{1,0:T(8,128)S(1)} %fusion.4, f32[800,128]{1,0:T(8,128)S(1)} %fusion.6, f32[800,128]{1,0:T(8,128)S(1)} %fusion.8), kind=kLoop, calls=%fused_computation.5 | loop fusion | flops 655360 | bytes 2621440 | tf_op jit(solution)/shard_map/concatenate | solution.py:92
  (58 shorter events, 3.9 us)
Async XLA Ops:
  0.0 5.3 %copy-start.8 = (s32[2560]{0:T(1024)S(1)}, s32[2560]{0:T(1024)}, u32[]{:S(2)}) copy-start(s32[2560]{0:T(1024)} %param.17) | copy-start | bytes 30724
  0.0 5.4 %copy-start.12 = (s32[2560]{0:T(1024)S(1)}, s32[2560]{0:T(1024)}, u32[]{:S(2)}) copy-start(s32[2560]{0:T(1024)} %param.18) | copy-start | bytes 30724
  0.0 5.5 %copy-start.16 = (bf16[3,64]{1,0:T(4,128)(2,1)S(1)}, bf16[3,64]{1,0:T(4,128)(2,1)}, u32[]{:S(2)}) copy-start(bf16[3,64]{1,0:T(4,128)(2,1)} %param.16) | copy-start | bytes 1156
  0.8 16.6 %copy-start.9 = (f32[2,800]{1,0:T(2,128)S(1)}, f32[2,800]{1,0:T(2,128)}, u32[]{:S(2)}) copy-start(f32[2,800]{1,0:T(2,128)} %param.20) | copy-start | bytes 19204
  0.8 16.6 %copy-start.10 = (f32[2,800]{1,0:T(2,128)S(1)}, f32[2,800]{1,0:T(2,128)}, u32[]{:S(2)}) copy-start(f32[2,800]{1,0:T(2,128)} %param.22) | copy-start | bytes 19204
  0.8 16.6 %copy-start.11 = (f32[2,800]{1,0:T(2,128)S(1)}, f32[2,800]{1,0:T(2,128)}, u32[]{:S(2)}) copy-start(f32[2,800]{1,0:T(2,128)} %param.21) | copy-start | bytes 19204
  0.8 17.2 %copy-start.13 = (f32[960]{0:T(1024)S(1)}, f32[960]{0:T(1024)}, u32[]{:S(2)}) copy-start(f32[960]{0:T(1024)} %param.25) | copy-start | bytes 11524
  0.9 17.2 %copy-start.14 = (f32[960]{0:T(1024)S(1)}, f32[960]{0:T(1024)}, u32[]{:S(2)}) copy-start(f32[960]{0:T(1024)} %param.23) | copy-start | bytes 11524
  0.9 17.2 %copy-start.15 = (f32[960]{0:T(1024)S(1)}, f32[960]{0:T(1024)}, u32[]{:S(2)}) copy-start(f32[960]{0:T(1024)} %param.24) | copy-start | bytes 11524
  2.3 15.8 %collective-permute-start = (bf16[1280,128]{1,0:T(8,128)(2,1)S(1)}, bf16[1280,128]{1,0:T(8,128)(2,1)S(1)}, u32[]{:S(2)}, u32[]{:S(2)}) collective-permute-start(bf16[1280,128]{1,0:T(8,128)(2,1)S(1)} %slice.182), channel_id=1, source_target_pairs={{0,2},{2,4},{4,6},{6,8},{8,10},{10,12},{12,14},{14,0},{1,3},{3,5},... | collective-permute-start | bytes 983048 | tf_op jit(solution)/shard_map/ppermute | solution.py:18
  31.5 6.2 %copy-start = (bf16[1600,800]{1,0:T(8,128)(2,1)S(1)}, bf16[1600,800]{1,0:T(8,128)(2,1)}, u32[]{:S(2)}) copy-start(bf16[1600,800]{1,0:T(8,128)(2,1)} %constant.12.clone) | copy-start | bytes 7680004
  37.6 1.9 %copy-start.4 = (bf16[2560,128]{1,0:T(8,128)(2,1)S(1)}, bf16[2560,128]{1,0:T(8,128)(2,1)}, u32[]{:S(2)}) copy-start(bf16[2560,128]{1,0:T(8,128)(2,1)} %gather_fusion) | copy-start | bytes 1966084
  39.6 1.4 %copy-start.2 = (bf16[800,800]{1,0:T(8,128)(2,1)S(1)}, bf16[800,800]{1,0:T(8,128)(2,1)}, u32[]{:S(2)}) copy-start(bf16[800,800]{1,0:T(8,128)(2,1)} %constant.87) | copy-start | bytes 3840004
  39.6 1.4 %copy-start.7 = (f32[800]{0:T(1024)S(1)}, f32[800]{0:T(1024)}, u32[]{:S(2)}) copy-start(f32[800]{0:T(1024)} %get-tuple-element.6) | copy-start | bytes 9604
  40.5 1.5 %copy-start.3 = (bf16[800,800]{1,0:T(8,128)(2,1)S(1)}, bf16[800,800]{1,0:T(8,128)(2,1)}, u32[]{:S(2)}) copy-start(bf16[800,800]{1,0:T(8,128)(2,1)} %constant.88) | copy-start | bytes 3840004
  42.7 2.1 %copy-start.1 = (bf16[1920,960]{1,0:T(8,128)(2,1)S(1)}, bf16[1920,960]{1,0:T(8,128)(2,1)}, u32[]{:S(2)}) copy-start(bf16[1920,960]{1,0:T(8,128)(2,1)} %constant.14.clone) | copy-start | bytes 11059204
  44.8 1.5 %copy-start.6 = (bf16[960,960]{1,0:T(8,128)(2,1)S(1)}, bf16[960,960]{1,0:T(8,128)(2,1)}, u32[]{:S(2)}) copy-start(bf16[960,960]{1,0:T(8,128)(2,1)} %constant.89) | copy-start | bytes 5529604
  46.4 1.5 %copy-start.5 = (bf16[960,960]{1,0:T(8,128)(2,1)S(1)}, bf16[960,960]{1,0:T(8,128)(2,1)}, u32[]{:S(2)}) copy-start(bf16[960,960]{1,0:T(8,128)(2,1)} %constant.90) | copy-start | bytes 5529604

commit v2 on v1

v2 whole, which is shorter than its diff:
```python
import functools
import math

import jax
import jax.numpy as jnp
import numpy as np
from jax import lax
from jax.experimental import pallas as pl
from jax.experimental.pallas import tpu as pltpu
from jax.sharding import PartitionSpec as P

LANES = 128
CHUNK = 256
MESH = pl.DeviceIdType.MESH
HIGHEST = lax.Precision.HIGHEST


def rounded_up(count):
    return -(-count // LANES) * LANES


def phase_tables(wire_count):
    padded = rounded_up(wire_count)
    columns = (padded - np.arange(2 * padded)) % wire_count
    multiples = np.concatenate([np.arange(LANES), LANES * np.arange(8)])
    turns = multiples[:, None] * columns[None, :] % wire_count
    angle = turns * (2.0 * math.pi / wire_count)
    return np.concatenate([np.cos(angle), np.sin(angle)], 1).astype(np.float32)


def strided(row):
    return pltpu.roll(jnp.broadcast_to(row, (LANES, LANES)), 0, 1, stride=1, stride_axis=0)


def kernel(
    induction,
    collection,
    waves,
    taps,
    slots,
    offsets,
    bad,
    induction_real,
    induction_imaginary,
    induction_filter,
    collection_real,
    collection_imaginary,
    collection_filter,
    induction_phases,
    collection_phases,
    out,
    halo,
    main,
    onehot,
    total,
    circulant_u,
    circulant_v,
    circulant_w,
    phases_uv,
    phases_w,
    spread,
    folded,
    rows_h,
    kernel_rows,
    result,
    next_send,
    near_send,
    far_send,
    halo_sem,
    main_sem,
    table_sem,
    out_sem,
):
    tm, apa = lax.axis_index("tm"), lax.axis_index("apa")
    windows = lax.axis_size("tm")
    following = lax.rem(tm + 1, windows)
    previous = lax.rem(tm + windows - 1, windows)
    pieces = waves.shape[0] // CHUNK
    padded_i, padded_c = rounded_up(induction), rounded_up(collection)
    bases = (0, padded_i, 2 * padded_i)
    sizes = (induction, induction, collection)

    barrier = pltpu.get_barrier_semaphore()

    def greet(window, core):
        pl.semaphore_signal(
            barrier, inc=1, device_id={"tm": window, "apa": core}, device_id_type=MESH
        )

    greet(tm, 1 - apa)

    @pl.when(apa == 0)
    def _():
        greet(previous, 0)
        greet(previous, 1)

    tables = [
        pltpu.make_async_copy(induction_phases, phases_uv, table_sem.at[0]),
        pltpu.make_async_copy(collection_phases, phases_w, table_sem.at[1]),
    ]
    pl.semaphore_wait(barrier, 2)

    def part(index, half):
        return waves.at[pl.ds(index * CHUNK, CHUNK), pl.ds(half * LANES, LANES)]

    def push(index, half, target, arrived, sent, window, core):
        return pltpu.make_async_remote_copy(
            src_ref=part(index, half),
            dst_ref=target,
            send_sem=sent,
            recv_sem=arrived,
            device_id={"tm": window, "apa": core},
            device_id_type=MESH,
        )

    def sends(core, kept=True):
        first = core * pieces
        ahead = [
            push(k, 1, halo.at[first + k], halo_sem.at[first + k], next_send.at[k], following, 0)
            for k in range(pieces)
        ]
        across, stay = [], []
        for k in range(pieces):
            spot = first + k
            if core == 0:
                across.append(
                    push(k, 0, halo.at[spot], halo_sem.at[spot], near_send.at[k], tm, 1)
                )
                across.append(
                    push(k, 1, main.at[spot], main_sem.at[spot], far_send.at[k], tm, 1)
                )
                kept and stay.append(pltpu.make_async_copy(part(k, 0), main.at[spot], main_sem.at[spot]))
            else:
                across.append(
                    push(k, 0, main.at[spot], main_sem.at[spot], near_send.at[k], tm, 0)
                )
                kept and stay.append(pltpu.make_async_copy(part(k, 0), halo.at[spot], halo_sem.at[spot]))
                kept and stay.append(pltpu.make_async_copy(part(k, 1), main.at[spot], main_sem.at[spot]))
        return ahead, across, stay

    for core in range(2):

        @pl.when(apa == core)
        def _():
            ahead, across, stay = sends(core)
            for copy in ahead + across + stay:
                copy.start()

    for copy in tables:
        copy.start()

    tile_rows = total.shape[0] // 11 if total.shape[0] % 11 == 0 else LANES
    lanes_row = lax.broadcasted_iota(jnp.int32, (tile_rows, CHUNK), 0)

    def make_onehot(index, carry):
        slot = slots[index]
        gap = padded_i - induction
        slot = slot + jnp.where(slot >= induction, gap, 0) + jnp.where(
            slot >= 2 * induction, gap, 0
        )
        slot = jnp.where(bad[index] == 0, slot, -1)
        for start in range(0, total.shape[0], tile_rows):
            hit = lanes_row == slot - start
            onehot[index, start : start + tile_rows, :] = jnp.where(hit, 1.0, 0.0).astype(
                jnp.bfloat16
            )
        return carry

    lax.fori_loop(0, 2 * pieces, make_onehot, 0)
    total[...] = jnp.zeros_like(total)

    spread[...] = jnp.zeros_like(spread)
    kernel_rows[...] = jnp.zeros_like(kernel_rows)
    kernel_rows[0:3, 0 : taps.shape[1]] = taps[...].astype(jnp.float32)
    for real, imaginary, gain, row in (
        (induction_real, induction_imaginary, induction_filter, 0),
        (collection_real, collection_imaginary, collection_filter, 4),
    ):
        count, width = real.shape
        re, im = real[...], imaginary[...]
        magnitude = re * re + im * im
        spread[row : row + count, 0:width] = gain[...] * re / magnitude
        spread[row + count : row + 2 * count, 0:width] = -gain[...] * im / magnitude
    for copy in tables:
        copy.wait()
    lane = lax.broadcasted_iota(jnp.int32, (LANES, LANES), 1)
    row_of = lax.broadcasted_iota(jnp.int32, (LANES, LANES), 0)
    for phases, count, first, targets, wires in (
        (phases_uv, 2, 0, (circulant_u, circulant_v), induction),
        (phases_w, 1, 4, (circulant_w,), collection),
    ):
        blocks = rounded_up(wires) // LANES
        length = 2 * blocks * LANES
        for entry in range(2 * count):
            for block in range(8):
                folded[8 * entry + block : 8 * entry + block + 1, :] = spread[
                    first + entry : first + entry + 1, block * LANES : (block + 1) * LANES
                ]
        terms = jnp.dot(
            folded[0 : 16 * count, :],
            phases[0:LANES, :],
            preferred_element_type=jnp.float32,
            precision=HIGHEST,
        )
        for entry in range(count):
            low, high = 8 * entry, 8 * (count + entry)
            re = terms[low : low + 8, :length] - terms[high : high + 8, length:]
            im = terms[low : low + 8, length:] + terms[high : high + 8, :length]
            turned = (
                phases[LANES : LANES + 8, :length] * re - phases[LANES : LANES + 8, length:] * im
            )
            rows_h[0:1, 0:length] = jnp.sum(turned, axis=0, keepdims=True) * (1.0 / wires)
            before = strided(rows_h[0:1, 0:LANES])
            for k in range(2 * blocks - 1):
                after = strided(rows_h[0:1, (k + 1) * LANES : (k + 2) * LANES])
                piece = jnp.where(lane >= row_of, after, before).astype(jnp.bfloat16)
                for i in range(blocks):
                    j = k - (blocks - 1) + i
                    if 0 <= j < blocks:
                        targets[entry][
                            i * LANES : (i + 1) * LANES, j * LANES : (j + 1) * LANES
                        ] = piece
                before = after

    def take(step, carry):
        index = lax.rem(step, 2) * pieces + step // 2
        pltpu.make_async_copy(main.at[index], main.at[index], main_sem.at[index]).wait()
        pltpu.make_async_copy(halo.at[index], halo.at[index], halo_sem.at[index]).wait()
        groups = []
        for start in range(0, CHUNK, LANES):
            delay = offsets[index, :, start : start + LANES].astype(jnp.float32)
            delay = jnp.broadcast_to(delay, (LANES, LANES)).T.astype(jnp.int32)
            origin = (lane - delay) & (LANES - 1)
            early = halo[index, start : start + LANES, :].astype(jnp.float32)
            late = main[index, start : start + LANES, :].astype(jnp.float32)
            early = jnp.take_along_axis(early, origin, axis=1)
            late = jnp.take_along_axis(late, origin, axis=1)
            late = jnp.where(lane >= delay, late, early)
            groups.append(jnp.concatenate([early, late], 1).astype(jnp.bfloat16))
        aligned = jnp.concatenate(groups, 0)
        for start in range(0, total.shape[0], tile_rows):
            total[start : start + tile_rows, :] += jnp.dot(
                onehot[index, start : start + tile_rows, :],
                aligned,
                preferred_element_type=jnp.float32,
            )
        return carry

    lax.fori_loop(0, 2 * pieces, take, 0)

    outs = []
    place = 0
    for plane, circulant in enumerate((circulant_u, circulant_v, circulant_w)):
        base, wires = bases[plane], sizes[plane]
        padded = rounded_up(wires)
        turned = strided(kernel_rows[plane : plane + 1, :])
        toeplitz = jnp.concatenate(
            [jnp.where(lane < row_of, turned, 0.0), jnp.where(lane >= row_of, turned, 0.0)], 0
        ).astype(jnp.bfloat16)
        filtered = jnp.dot(
            total[base : base + padded, :].astype(jnp.bfloat16),
            toeplitz,
            preferred_element_type=jnp.float32,
        ).astype(jnp.bfloat16)
        values = jnp.dot(circulant[...], filtered, preferred_element_type=jnp.float32)
        result[place : place + wires, :] = values[:wires]
        span = pl.ds(place, wires)
        outs.append(pltpu.make_async_copy(result.at[span], out.at[span], out_sem.at[plane]))
        outs[-1].start()
        place += wires
    for copy in outs:
        copy.wait()
    for core in range(2):

        @pl.when(apa == core)
        def _():
            ahead, across, stay = sends(core, False)
            for copy in ahead + across:
                copy.wait_send()


def local(
    waveforms,
    time_kernel,
    wire_slot,
    tick_offset,
    bad_channel,
    induction_real,
    induction_imaginary,
    induction_filter,
    collection_real,
    collection_imaginary,
    collection_filter,
):
    channels = wire_slot.shape[0]
    induction, collection = induction_real.shape[1], collection_real.shape[0]
    padded_i, padded_c = rounded_up(induction), rounded_up(collection)
    rows = 2 * padded_i + padded_c
    chunks = channels // CHUNK
    pieces = chunks // 2
    vmem, anywhere = pl.BlockSpec(memory_space=pltpu.VMEM), pl.BlockSpec(memory_space=pl.ANY)
    uv, w = phase_tables(induction), phase_tables(collection)
    return pl.pallas_call(
        functools.partial(kernel, induction, collection),
        out_shape=jax.ShapeDtypeStruct((channels, LANES), jnp.float32),
        in_specs=[anywhere] + [vmem] * 10 + [anywhere] * 2,
        out_specs=anywhere,
        scratch_shapes=[
            pltpu.VMEM((chunks, CHUNK, LANES), jnp.bfloat16),
            pltpu.VMEM((chunks, CHUNK, LANES), jnp.bfloat16),
            pltpu.VMEM((chunks, rows, CHUNK), jnp.bfloat16),
            pltpu.VMEM((rows, 2 * LANES), jnp.float32),
            pltpu.VMEM((padded_i, padded_i), jnp.bfloat16),
            pltpu.VMEM((padded_i, padded_i), jnp.bfloat16),
            pltpu.VMEM((padded_c, padded_c), jnp.bfloat16),
            pltpu.VMEM(uv.shape, jnp.float32),
            pltpu.VMEM(w.shape, jnp.float32),
            pltpu.VMEM((8, 8 * LANES), jnp.float32),
            pltpu.VMEM((32, LANES), jnp.float32),
            pltpu.VMEM((8, 2 * max(padded_i, padded_c)), jnp.float32),
            pltpu.VMEM((8, LANES), jnp.float32),
            pltpu.VMEM((channels, LANES), jnp.float32),
            pltpu.SemaphoreType.DMA((pieces,)),
            pltpu.SemaphoreType.DMA((pieces,)),
            pltpu.SemaphoreType.DMA((pieces,)),
            pltpu.SemaphoreType.DMA((chunks,)),
            pltpu.SemaphoreType.DMA((chunks,)),
            pltpu.SemaphoreType.DMA((2,)),
            pltpu.SemaphoreType.DMA((3,)),
        ],
        compiler_params=pltpu.CompilerParams(
            collective_id=0, has_side_effects=True, vmem_limit_bytes=48 * 1024 * 1024
        ),
    )(
        waveforms,
        time_kernel,
        wire_slot.reshape(chunks, 1, CHUNK),
        tick_offset.reshape(chunks, 1, CHUNK),
        bad_channel.reshape(chunks, 1, CHUNK),
        induction_real,
        induction_imaginary,
        induction_filter,
        collection_real.reshape(1, collection),
        collection_imaginary.reshape(1, collection),
        collection_filter.reshape(1, collection),
        uv,
        w,
    )


def solution(mesh):
    placed = (
        P(("grp", "apa"), "tm"),
        P(),
        P("grp"),
        P("grp"),
        P("grp"),
        P(),
        P(),
        P(),
        P(),
        P(),
        P(),
    )
    return jax.shard_map(
        local, mesh=mesh, in_specs=placed, out_specs=P("grp", ("tm", "apa")), check_vma=False
    )
```

time: 50.3 us -> 34.3 us (0.68)
  Pallas kernels: 0 us -> 21.3 us
  matrix products: 10.7 us -> 0 us
  other arithmetic: 10.2 us -> 0 us
  local copies, waits for them, and re-layouts: 21.4 us -> 12.3 us
  blocking collectives: 4.26 us -> 0 us
  starting transfers between devices: 2.99 us -> 0 us
    pallas_call x0 -> x1, Pallas kernels: none -> 21.3 us  [local(): pl.pallas_call(functools.partial(kernel, induction, collection), out_shap...]
    dot_general x15 -> x0, matrix products: 10.7 us -> none  [the longest x6 4.53 us: wire_deconvolve(): jnp.dot(backward, product, preferred_element_type=jnp.float32)]
    scatter x1 -> x0, local copies, waits for them, and re-layouts: 9.93 us -> none  [local(): inverse = jnp.zeros((channel_count,), jnp.int32).at[wire_slot].set(jnp.ar...]
    unnamed x34 -> x21, local copies, waits for them, and re-layouts: 2.53 us -> 10.1 us
    gather x1 -> x0, local copies, waits for them, and re-layouts: 6.14 us -> none  [local(): ordered = regrouped[inverse]]
    select_n x8 -> x0, other arithmetic: 5.6 us -> none  [the longest x6 5.6 us: shift_rows(): current = jnp.where(chosen[:, None], moved, current)]
    all_to_all x1 -> x0, blocking collectives: 4.26 us -> none  [local(): lax.all_to_all(filtered, 'apa', split_axis=1, concat_axis=0, tiled=True)]
    ppermute x1 -> x0, starting transfers between devices: 2.99 us -> none  [shifted(): return lax.ppermute(value, axis, pairs)]
  transfers between devices with their start and end apart: 1 -> 0, of which waited for: 0 -> 0; matrix products, arithmetic and copies ran while one was open for 25% -> 0% of each run, Pallas kernels for 0% -> 0%
where the time goes in v2:
time: 34.3 us; the launch traced here: 33.6 us
  Pallas kernels  21.3 us (62%)
  local copies, waits for them, and re-layouts  12.3 us (36%)
    pallas_call x1, Pallas kernels, local(): pl.pallas_call(functools.partial(kernel, induction, collection), out_shap...  21.3 us
    unnamed x21, local copies, waits for them, and re-layouts  10.1 us
    reshape x1, local copies, waits for them, and re-layouts, local(): tick_offset.reshape(chunks, 1, CHUNK)  0.72 us
    reshape x1, local copies, waits for them, and re-layouts, local(): bad_channel.reshape(chunks, 1, CHUNK)  0.72 us
    reshape x1, local copies, waits for them, and re-layouts, local(): wire_slot.reshape(chunks, 1, CHUNK)  0.72 us

profile of v2, /device:TPU:0, one launch (start us, length us, event | category | flops | bytes accessed | tf_op | source)
XLA Modules:
  0.0 33.6 jit_solution(8515938197145943000)
XLA Ops:
  0.0 0.7 %reshape.18.slots = s32[10,1,256]{2,1,0:T(1,128)S(1)} reshape(s32[2560]{0:T(1024)} %param.15) | data formatting | bytes 20480 | tf_op jit(solution)/shard_map/reshape | solution.py:337
  0.7 0.7 %reshape.19.offsets = s32[10,1,256]{2,1,0:T(1,128)S(1)} reshape(s32[2560]{0:T(1024)} %param.16) | data formatting | bytes 20480 | tf_op jit(solution)/shard_map/reshape | solution.py:338
  1.4 0.7 %reshape.20.bad = s32[10,1,256]{2,1,0:T(1,128)S(1)} reshape(s32[2560]{0:T(1024)} %param.17) | data formatting | bytes 20480 | tf_op jit(solution)/shard_map/reshape | solution.py:339
  2.2 0.0 copy-start
  2.2 1.6 %copy-done = f32[136,4096]{1,0:T(8,128)S(1)} copy-done((f32[136,4096]{1,0:T(8,128)S(1)}, f32[136,4096]{1,0:T(8,128)}, u32[]{:S(2)}) %copy-start) | copy-done | bytes 2228248
  3.8 0.0 copy-start.1
  3.8 1.5 %copy-done.1 = f32[136,3584]{1,0:T(8,128)S(1)} copy-done((f32[136,3584]{1,0:T(8,128)S(1)}, f32[136,3584]{1,0:T(8,128)}, u32[]{:S(2)}) %copy-start.1) | copy-done | bytes 1949720
  5.3 0.0 copy-start.2
  5.3 1.1 %copy-done.2 = bf16[1280,256]{1,0:T(8,128)(2,1)S(1)} copy-done((bf16[1280,256]{1,0:T(8,128)(2,1)S(1)}, bf16[1280,256]{1,0:T(8,128)(2,1)}, u32[]{:S(2)}) %copy-start.2) | copy-done | bytes 655384
  6.4 0.0 copy-start.3
  6.4 0.7 %copy-done.3 = f32[2,800]{1,0:T(2,128)S(1)} copy-done((f32[2,800]{1,0:T(2,128)S(1)}, f32[2,800]{1,0:T(2,128)}, u32[]{:S(2)}) %copy-start.3) | copy-done | bytes 6424
  7.1 0.0 copy-start.4
  7.1 0.7 %copy-done.4 = f32[2,800]{1,0:T(2,128)S(1)} copy-done((f32[2,800]{1,0:T(2,128)S(1)}, f32[2,800]{1,0:T(2,128)}, u32[]{:S(2)}) %copy-start.4) | copy-done | bytes 6424
  7.8 0.0 copy-start.5
  7.8 0.7 %copy-done.5 = f32[2,800]{1,0:T(2,128)S(1)} copy-done((f32[2,800]{1,0:T(2,128)S(1)}, f32[2,800]{1,0:T(2,128)}, u32[]{:S(2)}) %copy-start.5) | copy-done | bytes 6424
  8.5 0.0 copy-start.6
  8.5 0.7 %copy-done.6 = f32[960]{0:T(1024)S(1)} copy-done((f32[960]{0:T(1024)S(1)}, f32[960]{0:T(1024)}, u32[]{:S(2)}) %copy-start.6) | copy-done | bytes 3864
  9.2 0.0 copy-start.7
  9.2 0.7 %copy-done.7 = f32[960]{0:T(1024)S(1)} copy-done((f32[960]{0:T(1024)S(1)}, f32[960]{0:T(1024)}, u32[]{:S(2)}) %copy-start.7) | copy-done | bytes 3864
  9.9 0.0 copy-start.8
  9.9 0.7 %copy-done.8 = f32[960]{0:T(1024)S(1)} copy-done((f32[960]{0:T(1024)S(1)}, f32[960]{0:T(1024)}, u32[]{:S(2)}) %copy-start.8) | copy-done | bytes 3864
  10.6 0.0 copy-start.9
  10.6 0.7 %copy-done.9 = bf16[3,64]{1,0:T(4,128)(2,1)S(1)} copy-done((bf16[3,64]{1,0:T(4,128)(2,1)S(1)}, bf16[3,64]{1,0:T(4,128)(2,1)}, u32[]{:S(2)}) %copy-start.9) | copy-done | bytes 408
  11.2 21.3 %shard_map.127 = f32[2560,128]{1,0:T(8,128)S(1)} custom-call(bf16[1280,256]{1,0:T(8,128)(2,1)S(1)} %copy-done.2, bf16[3,64]{1,0:T(4,128)(2,1)S(1)} %copy-done.9, s32[10,1,256]{2,1,0:T(1,128)S(1)} %reshape.18.slots, s32[10,1,256]{2,1,0:T(1,128)S(1)} %reshape.19.offsets, s32[10,1,256]{2,1,0:T(1,128)S(1)} %reshape.20.bad, f32[2,800]{1,0:T(2,128)S(1)} %copy-done.3, ...), custom_call_target="tpu_custom_call" | custom-call | tf_op jit(solution)/shard_map/pallas_call | solution.py:303
  32.6 1.1 %copy.15 = f32[2560,128]{1,0:T(8,128)} copy(f32[2560,128]{1,0:T(8,128)S(1)} %shard_map.127) | data formatting | bytes 2621440
Async XLA Ops:
  2.2 1.6 %copy-start = (f32[136,4096]{1,0:T(8,128)S(1)}, f32[136,4096]{1,0:T(8,128)}, u32[]{:S(2)}) copy-start(f32[136,4096]{1,0:T(8,128)} %constant.5.clone.collection_phases) | copy-start | bytes 6684676
  3.8 1.5 %copy-start.1 = (f32[136,3584]{1,0:T(8,128)S(1)}, f32[136,3584]{1,0:T(8,128)}, u32[]{:S(2)}) copy-start(f32[136,3584]{1,0:T(8,128)} %constant.4.clone.induction_phases) | copy-start | bytes 5849092
  5.3 1.1 %copy-start.2 = (bf16[1280,256]{1,0:T(8,128)(2,1)S(1)}, bf16[1280,256]{1,0:T(8,128)(2,1)}, u32[]{:S(2)}) copy-start(bf16[1280,256]{1,0:T(8,128)(2,1)} %waves.1) | copy-start | bytes 1966084
  6.4 0.7 %copy-start.3 = (f32[2,800]{1,0:T(2,128)S(1)}, f32[2,800]{1,0:T(2,128)}, u32[]{:S(2)}) copy-start(f32[2,800]{1,0:T(2,128)} %induction_real.1) | copy-start | bytes 19204
  7.1 0.7 %copy-start.4 = (f32[2,800]{1,0:T(2,128)S(1)}, f32[2,800]{1,0:T(2,128)}, u32[]{:S(2)}) copy-start(f32[2,800]{1,0:T(2,128)} %induction_imaginary.1) | copy-start | bytes 19204
  7.8 0.7 %copy-start.5 = (f32[2,800]{1,0:T(2,128)S(1)}, f32[2,800]{1,0:T(2,128)}, u32[]{:S(2)}) copy-start(f32[2,800]{1,0:T(2,128)} %induction_filter.1) | copy-start | bytes 19204
  8.5 0.7 %copy-start.6 = (f32[960]{0:T(1024)S(1)}, f32[960]{0:T(1024)}, u32[]{:S(2)}) copy-start(f32[960]{0:T(1024)} %param.21) | copy-start | bytes 11524
  9.2 0.7 %copy-start.7 = (f32[960]{0:T(1024)S(1)}, f32[960]{0:T(1024)}, u32[]{:S(2)}) copy-start(f32[960]{0:T(1024)} %param.22) | copy-start | bytes 11524
  9.9 0.7 %copy-start.8 = (f32[960]{0:T(1024)S(1)}, f32[960]{0:T(1024)}, u32[]{:S(2)}) copy-start(f32[960]{0:T(1024)} %param.23) | copy-start | bytes 11524
  10.6 0.7 %copy-start.9 = (bf16[3,64]{1,0:T(4,128)(2,1)S(1)}, bf16[3,64]{1,0:T(4,128)(2,1)}, u32[]{:S(2)}) copy-start(bf16[3,64]{1,0:T(4,128)(2,1)} %taps.1) | copy-start | bytes 1156

commit v3 on v2

v3 whole, which is shorter than its diff:
```python
import functools
import math

import jax
import jax.numpy as jnp
import numpy as np
from jax import lax
from jax.experimental import pallas as pl
from jax.experimental.pallas import tpu as pltpu
from jax.sharding import PartitionSpec as P

LANES = 128
CHUNK = 256
MESH = pl.DeviceIdType.MESH


def rounded_up(count):
    return -(-count // LANES) * LANES


def phase_tables(wire_count):
    padded = rounded_up(wire_count)
    columns = (padded - np.arange(padded)) % wire_count

    def both(multiples):
        angle = (multiples[:, None] * columns[None, :] % wire_count) * (2.0 * math.pi / wire_count)
        return np.concatenate([np.cos(angle), np.sin(angle)], 0)

    fine, coarse = both(np.arange(LANES)), both(LANES * np.arange(8))
    return fine.astype(np.float32), coarse.astype(np.float32)


def halves(values):
    high = values.astype(jnp.bfloat16)
    return high, (values - high.astype(jnp.float32)).astype(jnp.bfloat16)


def strided(row):
    return pltpu.roll(jnp.broadcast_to(row, (LANES, LANES)), 0, 1, stride=1, stride_axis=0)


def kernel(induction, collection, waves, *refs):
    operands, out, copies = refs[:14], refs[14], refs[15:29]
    (
        halo,
        main,
        onehot,
        total,
        circulant_u,
        circulant_v,
        circulant_w,
        spread,
        folded,
        rows_h,
        kernel_rows,
        result,
        next_send,
        near_send,
        far_send,
        halo_sem,
        main_sem,
        fetch_sem,
        out_sem,
    ) = refs[29:]
    (
        taps,
        slots,
        offsets,
        bad,
        induction_real,
        induction_imaginary,
        induction_filter,
        collection_real,
        collection_imaginary,
        collection_filter,
        fine_uv,
        coarse_uv,
        fine_w,
        coarse_w,
    ) = copies
    tm, apa = lax.axis_index("tm"), lax.axis_index("apa")
    windows = lax.axis_size("tm")
    following = lax.rem(tm + 1, windows)
    previous = lax.rem(tm + windows - 1, windows)
    pieces = waves.shape[0] // CHUNK
    padded_i, padded_c = rounded_up(induction), rounded_up(collection)
    bases = (0, padded_i, 2 * padded_i)
    sizes = (induction, induction, collection)

    barrier = pltpu.get_barrier_semaphore()

    def greet(window, core):
        pl.semaphore_signal(
            barrier, inc=1, device_id={"tm": window, "apa": core}, device_id_type=MESH
        )

    greet(tm, 1 - apa)

    @pl.when(apa == 0)
    def _():
        greet(previous, 0)
        greet(previous, 1)

    fetches = [
        pltpu.make_async_copy(source, copy, fetch_sem.at[number])
        for number, (source, copy) in enumerate(zip(operands, copies))
    ]
    for fetch in fetches[:10]:
        fetch.start()
    pl.semaphore_wait(barrier, 2)

    def part(index, half):
        return waves.at[pl.ds(index * CHUNK, CHUNK), pl.ds(half * LANES, LANES)]

    def push(index, half, target, arrived, sent, window, core):
        return pltpu.make_async_remote_copy(
            src_ref=part(index, half),
            dst_ref=target,
            send_sem=sent,
            recv_sem=arrived,
            device_id={"tm": window, "apa": core},
            device_id_type=MESH,
        )

    def sends(core, kept=True):
        first = core * pieces
        ahead = [
            push(k, 1, halo.at[first + k], halo_sem.at[first + k], next_send.at[k], following, 0)
            for k in range(pieces)
        ]
        across, stay = [], []
        for k in range(pieces):
            spot = first + k
            if core == 0:
                across.append(
                    push(k, 0, halo.at[spot], halo_sem.at[spot], near_send.at[k], tm, 1)
                )
                across.append(
                    push(k, 1, main.at[spot], main_sem.at[spot], far_send.at[k], tm, 1)
                )
                kept and stay.append(pltpu.make_async_copy(part(k, 0), main.at[spot], main_sem.at[spot]))
            else:
                across.append(
                    push(k, 0, main.at[spot], main_sem.at[spot], near_send.at[k], tm, 0)
                )
                kept and stay.append(pltpu.make_async_copy(part(k, 0), halo.at[spot], halo_sem.at[spot]))
                kept and stay.append(pltpu.make_async_copy(part(k, 1), main.at[spot], main_sem.at[spot]))
        return ahead, across, stay

    for core in range(2):

        @pl.when(apa == core)
        def _():
            ahead, across, stay = sends(core)
            for copy in ahead + across + stay:
                copy.start()

    for fetch in fetches[10:]:
        fetch.start()
    for fetch in fetches[:10]:
        fetch.wait()

    build_rows = math.gcd(total.shape[0], 256)
    counted = lax.broadcasted_iota(jnp.int32, (build_rows, 2 * CHUNK), 0).astype(jnp.int16)
    one, zero = jnp.bfloat16(1), jnp.bfloat16(0)

    def span_of(ref, first, count):
        return ref[:, pl.ds(pl.multiple_of(first, LANES), count)]

    def joined(ref, step):
        return jnp.concatenate(
            [span_of(ref, index * CHUNK, CHUNK) for index in (step, pieces + step)], 1
        )

    def make_onehot(step, carry):
        slot = joined(slots, step)
        gap = padded_i - induction
        slot = slot + jnp.where(slot >= induction, gap, 0) + jnp.where(
            slot >= 2 * induction, gap, 0
        )
        slot = jnp.where(joined(bad, step) == 0, slot, -1)
        for start in range(0, total.shape[0], build_rows):
            hit = counted == (slot - start).astype(jnp.int16)
            onehot[step, start : start + build_rows, :] = jnp.where(hit, one, zero)
        return carry

    lax.fori_loop(0, pieces, make_onehot, 0)
    total[...] = jnp.zeros_like(total)

    spread[...] = jnp.zeros_like(spread)
    kernel_rows[...] = jnp.zeros_like(kernel_rows)
    kernel_rows[0:3, 0 : taps.shape[1]] = taps[...].astype(jnp.float32)
    for real, imaginary, gain, row in (
        (induction_real, induction_imaginary, induction_filter, 0),
        (collection_real, collection_imaginary, collection_filter, 4),
    ):
        count, width = real.shape
        re, im = real[...], imaginary[...]
        magnitude = re * re + im * im
        spread[row : row + count, 0:width] = gain[...] * re / magnitude
        spread[row + count : row + 2 * count, 0:width] = -gain[...] * im / magnitude
    for fetch in fetches[10:]:
        fetch.wait()
    lane = lax.broadcasted_iota(jnp.int32, (LANES, LANES), 1)
    row_of = lax.broadcasted_iota(jnp.int32, (LANES, LANES), 0)
    for fine, coarse, count, first, targets, wires in (
        (fine_uv, coarse_uv, 2, 0, (circulant_u, circulant_v), induction),
        (fine_w, coarse_w, 1, 4, (circulant_w,), collection),
    ):
        padded = rounded_up(wires)
        blocks = padded // LANES
        for entry in range(count):
            for block in range(8):
                columns = slice(block * LANES, (block + 1) * LANES)
                re = spread[first + entry : first + entry + 1, columns]
                im = spread[first + count + entry : first + count + entry + 1, columns]
                row = 16 * entry + block
                folded[row : row + 1, 0:LANES] = re
                folded[row : row + 1, LANES : 2 * LANES] = -im
                folded[row + 8 : row + 9, 0:LANES] = im
                folded[row + 8 : row + 9, LANES : 2 * LANES] = re
        both = jnp.concatenate(halves(folded[0 : 16 * count, :]), 0)
        terms = sum(
            jnp.dot(both, table, preferred_element_type=jnp.float32) for table in halves(fine[...])
        )
        terms = terms[: 16 * count] + terms[16 * count :]
        for entry in range(count):
            re = terms[16 * entry : 16 * entry + 8]
            im = terms[16 * entry + 8 : 16 * entry + 16]
            turned = coarse[0:8, :] * re - coarse[8:16, :] * im
            line = jnp.sum(turned, axis=0, keepdims=True) * (1.0 / wires)
            rows_h[0:1, 0:padded] = line
            rows_h[0:1, wires : wires + padded] = line
            if padded > wires:
                rows_h[0:1, 2 * wires : 2 * padded] = line[:, : 2 * (padded - wires)]
            before = strided(rows_h[0:1, 0:LANES])
            for k in range(2 * blocks - 1):
                after = strided(rows_h[0:1, (k + 1) * LANES : (k + 2) * LANES])
                piece = jnp.where(lane >= row_of, after, before).astype(jnp.bfloat16)
                for i in range(blocks):
                    j = k - (blocks - 1) + i
                    if 0 <= j < blocks:
                        targets[entry][
                            i * LANES : (i + 1) * LANES, j * LANES : (j + 1) * LANES
                        ] = piece
                before = after

    tile_rows = total.shape[0] // 2

    def take(step, carry):
        groups = []
        for index in (step, pieces + step):
            pltpu.make_async_copy(main.at[index], main.at[index], main_sem.at[index]).wait()
            pltpu.make_async_copy(halo.at[index], halo.at[index], halo_sem.at[index]).wait()
        for index in (step, pieces + step):
            for start in range(0, CHUNK, LANES):
                delay = span_of(offsets, index * CHUNK + start, LANES).astype(jnp.float32)
                delay = jnp.broadcast_to(delay, (LANES, LANES)).T.astype(jnp.int32)
                origin = (lane - delay) & (LANES - 1)
                early = halo[index, start : start + LANES, :].astype(jnp.float32)
                late = main[index, start : start + LANES, :].astype(jnp.float32)
                early = jnp.take_along_axis(early, origin, axis=1)
                late = jnp.take_along_axis(late, origin, axis=1)
                late = jnp.where(lane >= delay, late, early)
                groups.append(jnp.concatenate([early, late], 1).astype(jnp.bfloat16))
        aligned = jnp.concatenate(groups, 0)
        for start in range(0, total.shape[0], tile_rows):
            total[start : start + tile_rows, :] += jnp.dot(
                onehot[step, start : start + tile_rows, :],
                aligned,
                preferred_element_type=jnp.float32,
            )
        return carry

    lax.fori_loop(0, pieces, take, 0)

    outs = []
    place = 0
    for plane, circulant in enumerate((circulant_u, circulant_v, circulant_w)):
        base, wires = bases[plane], sizes[plane]
        padded = rounded_up(wires)
        turned = strided(kernel_rows[plane : plane + 1, :])
        toeplitz = jnp.concatenate(
            [jnp.where(lane < row_of, turned, 0.0), jnp.where(lane >= row_of, turned, 0.0)], 0
        ).astype(jnp.bfloat16)
        filtered = jnp.dot(
            total[base : base + padded, :].astype(jnp.bfloat16),
            toeplitz,
            preferred_element_type=jnp.float32,
        ).astype(jnp.bfloat16)
        values = jnp.dot(circulant[...], filtered, preferred_element_type=jnp.float32)
        result[place : place + wires, :] = values[:wires]
        span = pl.ds(place, wires)
        outs.append(pltpu.make_async_copy(result.at[span], out.at[span], out_sem.at[plane]))
        outs[-1].start()
        place += wires
    for copy in outs:
        copy.wait()
    for core in range(2):

        @pl.when(apa == core)
        def _():
            ahead, across, stay = sends(core, False)
            for copy in ahead + across:
                copy.wait_send()


def local(
    waveforms,
    time_kernel,
    wire_slot,
    tick_offset,
    bad_channel,
    induction_real,
    induction_imaginary,
    induction_filter,
    collection_real,
    collection_imaginary,
    collection_filter,
):
    channels = wire_slot.shape[0]
    induction, collection = induction_real.shape[1], collection_real.shape[0]
    padded_i, padded_c = rounded_up(induction), rounded_up(collection)
    rows = 2 * padded_i + padded_c
    chunks = channels // CHUNK
    pieces = chunks // 2
    split = (1, channels)
    operands = [
        time_kernel,
        wire_slot.reshape(split),
        tick_offset.reshape(split),
        bad_channel.reshape(split),
        induction_real,
        induction_imaginary,
        induction_filter,
        collection_real.reshape(1, collection),
        collection_imaginary.reshape(1, collection),
        collection_filter.reshape(1, collection),
        *phase_tables(induction),
        *phase_tables(collection),
    ]
    far = pl.BlockSpec(memory_space=pltpu.HBM)
    return pl.pallas_call(
        functools.partial(kernel, induction, collection),
        out_shape=jax.ShapeDtypeStruct((channels, LANES), jnp.float32),
        in_specs=[far] * (1 + len(operands)),
        out_specs=far,
        scratch_shapes=[pltpu.VMEM(operand.shape, operand.dtype) for operand in operands]
        + [
            pltpu.VMEM((chunks, CHUNK, LANES), jnp.bfloat16),
            pltpu.VMEM((chunks, CHUNK, LANES), jnp.bfloat16),
            pltpu.VMEM((pieces, rows, 2 * CHUNK), jnp.bfloat16),
            pltpu.VMEM((rows, 2 * LANES), jnp.float32),
            pltpu.VMEM((padded_i, padded_i), jnp.bfloat16),
            pltpu.VMEM((padded_i, padded_i), jnp.bfloat16),
            pltpu.VMEM((padded_c, padded_c), jnp.bfloat16),
            pltpu.VMEM((8, 8 * LANES), jnp.float32),
            pltpu.VMEM((32, 2 * LANES), jnp.float32),
            pltpu.VMEM((8, 2 * max(padded_i, padded_c)), jnp.float32),
            pltpu.VMEM((8, LANES), jnp.float32),
            pltpu.VMEM((channels, LANES), jnp.float32),
            pltpu.SemaphoreType.DMA((pieces,)),
            pltpu.SemaphoreType.DMA((pieces,)),
            pltpu.SemaphoreType.DMA((pieces,)),
            pltpu.SemaphoreType.DMA((chunks,)),
            pltpu.SemaphoreType.DMA((chunks,)),
            pltpu.SemaphoreType.DMA((len(operands),)),
            pltpu.SemaphoreType.DMA((3,)),
        ],
        compiler_params=pltpu.CompilerParams(
            collective_id=0, has_side_effects=True, vmem_limit_bytes=62 * 1024 * 1024
        ),
    )(waveforms, *operands)


def solution(mesh):
    placed = (
        P(("grp", "apa"), "tm"),
        P(),
        P("grp"),
        P("grp"),
        P("grp"),
        P(),
        P(),
        P(),
        P(),
        P(),
        P(),
    )
    return jax.shard_map(
        local, mesh=mesh, in_specs=placed, out_specs=P("grp", ("tm", "apa")), check_vma=False
    )
```

time: 34.3 us -> 26.7 us (0.78)
  local copies, waits for them, and re-layouts: 12.3 us -> 6.39 us
  Pallas kernels: 21.3 us -> 19.9 us
    unnamed x21 -> x1, local copies, waits for them, and re-layouts: 10.1 us -> 2.46 us
    reshape x3, local copies, waits for them, and re-layouts: 2.16 us -> 3.93 us  [the longest x1 1.31 us: local(): wire_slot.reshape(split)]
    pallas_call x1, Pallas kernels: 21.3 us -> 19.9 us  [local(): pl.pallas_call(functools.partial(kernel, induction, collection), out_shap...]
where the time goes in v3:
time: 26.7 us; the launch traced here: 26.3 us
  Pallas kernels  19.9 us (75%)
  local copies, waits for them, and re-layouts  6.39 us (24%)
    pallas_call x1, Pallas kernels, local(): pl.pallas_call(functools.partial(kernel, induction, collection), out_shap...  19.9 us
    unnamed x1, local copies, waits for them, and re-layouts  2.46 us
    reshape x1, local copies, waits for them, and re-layouts, local(): wire_slot.reshape(split)  1.31 us
    reshape x1, local copies, waits for them, and re-layouts, local(): tick_offset.reshape(split)  1.31 us
    reshape x1, local copies, waits for them, and re-layouts, local(): bad_channel.reshape(split)  1.31 us

profile of v3, /device:TPU:0, one launch (start us, length us, event | category | flops | bytes accessed | tf_op | source)
XLA Modules:
  0.0 26.3 jit_solution(3274203647422862006)
XLA Ops:
  0.0 1.3 %reshape.18.refs_1_ = s32[1,2560]{1,0:T(1,128)} reshape(s32[2560]{0:T(1024)} %param.17) | data formatting | bytes 20480 | tf_op jit(solution)/shard_map/reshape | solution.py:330
  1.3 1.3 %reshape.19.refs_2_ = s32[1,2560]{1,0:T(1,128)} reshape(s32[2560]{0:T(1024)} %param.18) | data formatting | bytes 20480 | tf_op jit(solution)/shard_map/reshape | solution.py:331
  2.6 1.3 %reshape.20.refs_3_ = s32[1,2560]{1,0:T(1,128)} reshape(s32[2560]{0:T(1024)} %param.19) | data formatting | bytes 20480 | tf_op jit(solution)/shard_map/reshape | solution.py:332
  3.9 19.9 %shard_map.145 = f32[2560,128]{1,0:T(8,128)} custom-call(bf16[1280,256]{1,0:T(8,128)(2,1)} %waves.1, bf16[3,64]{1,0:T(4,128)(2,1)} %refs_0_.1, s32[1,2560]{1,0:T(1,128)} %reshape.18.refs_1_, s32[1,2560]{1,0:T(1,128)} %reshape.19.refs_2_, s32[1,2560]{1,0:T(1,128)} %reshape.20.refs_3_, f32[2,800]{1,0:T(2,128)} %refs_4_.1, f32[2,800]{1,0:T(2,128)} %refs_5_.1, ...), custom_call_target="tpu_custom_call" | custom-call | tf_op jit(solution)/shard_map/pallas_call | solution.py:343
  23.9 2.5 %copy.17 = f32[2560,128]{1,0:T(8,128)} copy(f32[2560,128]{1,0:T(8,128)} %shard_map.145) | data formatting | bytes 2621440

commit v4 on v3

--- a/solution.py
+++ b/solution.py
@@ -10,7 +10,7 @@
 from jax.sharding import PartitionSpec as P
 
 LANES = 128
-CHUNK = 256
+CHUNK = 128
 MESH = pl.DeviceIdType.MESH
 
 
@@ -53,6 +53,7 @@
         folded,
         rows_h,
         kernel_rows,
+        toeplitz,
         result,
         next_send,
         near_send,
@@ -83,9 +84,8 @@
     following = lax.rem(tm + 1, windows)
     previous = lax.rem(tm + windows - 1, windows)
     pieces = waves.shape[0] // CHUNK
-    padded_i, padded_c = rounded_up(induction), rounded_up(collection)
-    bases = (0, padded_i, 2 * padded_i)
     sizes = (induction, induction, collection)
+    starts = (0, induction, 2 * induction)
 
     barrier = pltpu.get_barrier_semaphore()
 
@@ -165,7 +165,7 @@
     one, zero = jnp.bfloat16(1), jnp.bfloat16(0)
 
     def span_of(ref, first, count):
-        return ref[:, pl.ds(pl.multiple_of(first, LANES), count)]
+        return ref[pl.ds(pl.multiple_of(first, LANES), count)].reshape(1, count)
 
     def joined(ref, step):
         return jnp.concatenate(
@@ -174,10 +174,6 @@
 
     def make_onehot(step, carry):
         slot = joined(slots, step)
-        gap = padded_i - induction
-        slot = slot + jnp.where(slot >= induction, gap, 0) + jnp.where(
-            slot >= 2 * induction, gap, 0
-        )
         slot = jnp.where(joined(bad, step) == 0, slot, -1)
         for start in range(0, total.shape[0], build_rows):
             hit = counted == (slot - start).astype(jnp.int16)
@@ -237,7 +233,7 @@
             for k in range(2 * blocks - 1):
                 after = strided(rows_h[0:1, (k + 1) * LANES : (k + 2) * LANES])
                 piece = jnp.where(lane >= row_of, after, before).astype(jnp.bfloat16)
-                for i in range(blocks):
+                for i in range(targets[entry].shape[0] // LANES):
                     j = k - (blocks - 1) + i
                     if 0 <= j < blocks:
                         targets[entry][
@@ -245,7 +241,13 @@
                         ] = piece
                 before = after
 
-    tile_rows = total.shape[0] // 2
+    for plane in range(3):
+        turned = strided(kernel_rows[plane : plane + 1, :])
+        columns = slice(plane * LANES, (plane + 1) * LANES)
+        toeplitz[0:LANES, columns] = jnp.where(lane < row_of, turned, 0.0).astype(jnp.bfloat16)
+        toeplitz[LANES : 2 * LANES, columns] = jnp.where(lane >= row_of, turned, 0.0).astype(
+            jnp.bfloat16
+        )
 
     def take(step, carry):
         groups = []
@@ -264,10 +266,13 @@
                 late = jnp.where(lane >= delay, late, early)
                 groups.append(jnp.concatenate([early, late], 1).astype(jnp.bfloat16))
         aligned = jnp.concatenate(groups, 0)
-        for start in range(0, total.shape[0], tile_rows):
-            total[start : start + tile_rows, :] += jnp.dot(
-                onehot[step, start : start + tile_rows, :],
-                aligned,
+        filtered = jnp.dot(aligned, toeplitz[...], preferred_element_type=jnp.float32).astype(
+            jnp.bfloat16
+        )
+        for plane, (start, wires) in enumerate(zip(starts, sizes)):
+            total[start : start + wires, :] += jnp.dot(
+                onehot[step, start : start + wires, :],
+                filtered[:, plane * LANES : (plane + 1) * LANES],
                 preferred_element_type=jnp.float32,
             )
         return carry
@@ -275,25 +280,24 @@
     lax.fori_loop(0, pieces, take, 0)
 
     outs = []
-    place = 0
     for plane, circulant in enumerate((circulant_u, circulant_v, circulant_w)):
-        base, wires = bases[plane], sizes[plane]
-        padded = rounded_up(wires)
-        turned = strided(kernel_rows[plane : plane + 1, :])
-        toeplitz = jnp.concatenate(
-            [jnp.where(lane < row_of, turned, 0.0), jnp.where(lane >= row_of, turned, 0.0)], 0
-        ).astype(jnp.bfloat16)
-        filtered = jnp.dot(
-            total[base : base + padded, :].astype(jnp.bfloat16),
-            toeplitz,
+        start, wires = starts[plane], sizes[plane]
+        half, spare = wires // 2, rounded_up(wires) - wires
+        top = total[start : start + half, :].astype(jnp.bfloat16)
+        bottom = total[start + half : start + wires, :].astype(jnp.bfloat16)
+        stacked = [jnp.concatenate([top, bottom], 1), jnp.concatenate([bottom, top], 1)]
+        if spare:
+            stacked.append(jnp.zeros((spare, 2 * LANES), jnp.bfloat16))
+        values = jnp.dot(
+            circulant[0:half, :],
+            jnp.concatenate(stacked, 0),
             preferred_element_type=jnp.float32,
-        ).astype(jnp.bfloat16)
-        values = jnp.dot(circulant[...], filtered, preferred_element_type=jnp.float32)
-        result[place : place + wires, :] = values[:wires]
-        span = pl.ds(place, wires)
+        )
+        result[start : start + half, :] = values[:, 0:LANES]
+        result[start + half : start + wires, :] = values[:, LANES:]
+        span = pl.ds(start, wires)
         outs.append(pltpu.make_async_copy(result.at[span], out.at[span], out_sem.at[plane]))
         outs[-1].start()
-        place += wires
     for copy in outs:
         copy.wait()
     for core in range(2):
@@ -303,6 +307,21 @@
             ahead, across, stay = sends(core, False)
             for copy in ahead + across:
                 copy.wait_send()
+
+
+def hand_over(found, out, sems):
+    pieces = sems.shape[0]
+    rows = found.shape[0] // pieces
+    copies = [
+        pltpu.make_async_copy(
+            found.at[pl.ds(k * rows, rows)], out.at[pl.ds(k * rows, rows)], sems.at[k]
+        )
+        for k in range(pieces)
+    ]
+    for copy in copies:
+        copy.start()
+    for copy in copies:
+        copy.wait()
 
 
 def local(
@@ -321,15 +340,14 @@
     channels = wire_slot.shape[0]
     induction, collection = induction_real.shape[1], collection_real.shape[0]
     padded_i, padded_c = rounded_up(induction), rounded_up(collection)
-    rows = 2 * padded_i + padded_c
+    half_i, half_c = rounded_up(induction // 2), rounded_up(collection // 2)
     chunks = channels // CHUNK
     pieces = chunks // 2
-    split = (1, channels)
     operands = [
         time_kernel,
-        wire_slot.reshape(split),
-        tick_offset.reshape(split),
-        bad_channel.reshape(split),
+        wire_slot,
+        tick_offset,
+        bad_channel,
         induction_real,
         induction_imaginary,
         induction_filter,
@@ -340,7 +358,7 @@
         *phase_tables(collection),
     ]
     far = pl.BlockSpec(memory_space=pltpu.HBM)
-    return pl.pallas_call(
+    found = pl.pallas_call(
         functools.partial(kernel, induction, collection),
         out_shape=jax.ShapeDtypeStruct((channels, LANES), jnp.float32),
         in_specs=[far] * (1 + len(operands)),
@@ -349,15 +367,16 @@
         + [
             pltpu.VMEM((chunks, CHUNK, LANES), jnp.bfloat16),
             pltpu.VMEM((chunks, CHUNK, LANES), jnp.bfloat16),
-            pltpu.VMEM((pieces, rows, 2 * CHUNK), jnp.bfloat16),
-            pltpu.VMEM((rows, 2 * LANES), jnp.float32),
-            pltpu.VMEM((padded_i, padded_i), jnp.bfloat16),
-            pltpu.VMEM((padded_i, padded_i), jnp.bfloat16),
-            pltpu.VMEM((padded_c, padded_c), jnp.bfloat16),
+            pltpu.VMEM((pieces, channels, 2 * CHUNK), jnp.bfloat16),
+            pltpu.VMEM((channels, LANES), jnp.float32),
+            pltpu.VMEM((half_i, padded_i), jnp.bfloat16),
+            pltpu.VMEM((half_i, padded_i), jnp.bfloat16),
+            pltpu.VMEM((half_c, padded_c), jnp.bfloat16),
             pltpu.VMEM((8, 8 * LANES), jnp.float32),
             pltpu.VMEM((32, 2 * LANES), jnp.float32),
             pltpu.VMEM((8, 2 * max(padded_i, padded_c)), jnp.float32),
             pltpu.VMEM((8, LANES), jnp.float32),
+            pltpu.VMEM((2 * LANES, 3 * LANES), jnp.bfloat16),
             pltpu.VMEM((channels, LANES), jnp.float32),
             pltpu.SemaphoreType.DMA((pieces,)),
             pltpu.SemaphoreType.DMA((pieces,)),
@@ -371,6 +390,14 @@
             collective_id=0, has_side_effects=True, vmem_limit_bytes=62 * 1024 * 1024
         ),
     )(waveforms, *operands)
+    return pl.pallas_call(
+        hand_over,
+        out_shape=jax.ShapeDtypeStruct(found.shape, found.dtype),
+        in_specs=[far],
+        out_specs=far,
+        scratch_shapes=[pltpu.SemaphoreType.DMA((8,))],
+        compiler_params=pltpu.CompilerParams(vmem_limit_bytes=62 * 1024 * 1024),
+    )(found)
 
 
 def solution(mesh):

time: 26.7 us -> 61.2 us (2.29)
  Pallas kernels: 19.9 us -> 61.1 us
  local copies, waits for them, and re-layouts: 6.39 us -> 0 us
    pallas_call x0 -> x1, Pallas kernels: none -> 40.9 us  [local(): pl.pallas_call(hand_over, out_shape=jax.ShapeDtypeStruct(found.shape, fou...]
    reshape x3 -> x0, local copies, waits for them, and re-layouts: 3.93 us -> none  [the longest x1 1.31 us: local(): wire_slot.reshape(split)]
    unnamed x1 -> x0, local copies, waits for them, and re-layouts: 2.46 us -> none
where the time goes in v4:
time: 61.2 us; the launch traced here: 61.1 us
  Pallas kernels  61.1 us (100%)
    pallas_call x1, Pallas kernels, local(): pl.pallas_call(hand_over, out_shape=jax.ShapeDtypeStruct(found.shape, fou...  40.9 us
    pallas_call x1, Pallas kernels, local(): pl.pallas_call(functools.partial(kernel, induction, collection), out_shap...  20.2 us

profile of v4, /device:TPU:0, one launch (start us, length us, event | category | flops | bytes accessed | tf_op | source)
XLA Modules:
  0.0 61.1 jit_solution(4559877300409477413)
XLA Ops:
  0.0 20.2 %shard_map.145.found = f32[2560,128]{1,0:T(8,128)} custom-call(bf16[1280,256]{1,0:T(8,128)(2,1)} %waves.1, bf16[3,64]{1,0:T(4,128)(2,1)} %refs_0_.1, s32[2560]{0:T(1024)} %refs_1_.1, s32[2560]{0:T(1024)} %refs_2_.1, s32[2560]{0:T(1024)} %refs_3_.1, f32[2,800]{1,0:T(2,128)} %refs_4_.1, f32[2,800]{1,0:T(2,128)} %refs_5_.1, f32[2,800]{1,0:T(2,128)} %refs_6_.1, ...), custom_call_target="tpu_custom_call" | custom-call | tf_op jit(solution)/shard_map/pallas_call | solution.py:361
  20.2 40.9 %shard_map.146 = f32[2560,128]{1,0:T(8,128)} custom-call(f32[2560,128]{1,0:T(8,128)} %shard_map.145.found), custom_call_target="tpu_custom_call" | custom-call | tf_op jit(solution)/shard_map/pallas_call | solution.py:393

commit v5 on v4

--- a/solution.py
+++ b/solution.py
@@ -10,7 +10,7 @@
 from jax.sharding import PartitionSpec as P
 
 LANES = 128
-CHUNK = 128
+CHUNK = 256
 MESH = pl.DeviceIdType.MESH
 
 
@@ -44,7 +44,8 @@
     (
         halo,
         main,
-        onehot,
+        staged,
+        origins,
         total,
         circulant_u,
         circulant_v,
@@ -60,6 +61,7 @@
         far_send,
         halo_sem,
         main_sem,
+        own_sem,
         fetch_sem,
         out_sem,
     ) = refs[29:]
@@ -105,16 +107,33 @@
         pltpu.make_async_copy(source, copy, fetch_sem.at[number])
         for number, (source, copy) in enumerate(zip(operands, copies))
     ]
+    def own_halves(core):
+        copies = ([], [])
+        for k in range(pieces):
+            spot = core * pieces + k
+            targets = (halo.at[spot], main.at[spot]) if core else (main.at[spot], staged.at[k])
+            for half in range(2):
+                source = waves.at[pl.ds(k * CHUNK, CHUNK), pl.ds(half * LANES, LANES)]
+                copies[half].append(
+                    pltpu.make_async_copy(source, targets[half], own_sem.at[half, k])
+                )
+        return copies
+
+    for core in range(2):
+
+        @pl.when(apa == core)
+        def _():
+            firsts, seconds = own_halves(core)
+            for copy in seconds + firsts:
+                copy.start()
+
     for fetch in fetches[:10]:
         fetch.start()
     pl.semaphore_wait(barrier, 2)
 
-    def part(index, half):
-        return waves.at[pl.ds(index * CHUNK, CHUNK), pl.ds(half * LANES, LANES)]
-
-    def push(index, half, target, arrived, sent, window, core):
+    def push(source, target, arrived, sent, window, core):
         return pltpu.make_async_remote_copy(
-            src_ref=part(index, half),
+            src_ref=source,
             dst_ref=target,
             send_sem=sent,
             recv_sem=arrived,
@@ -122,47 +141,51 @@
             device_id_type=MESH,
         )
 
-    def sends(core, kept=True):
-        first = core * pieces
-        ahead = [
-            push(k, 1, halo.at[first + k], halo_sem.at[first + k], next_send.at[k], following, 0)
-            for k in range(pieces)
-        ]
-        across, stay = [], []
+    def sends(core):
+        ahead, across = [], []
         for k in range(pieces):
-            spot = first + k
+            spot = core * pieces + k
+            second = main.at[spot] if core else staged.at[k]
+            ahead.append(
+                push(second, halo.at[spot], halo_sem.at[spot], next_send.at[k], following, 0)
+            )
             if core == 0:
                 across.append(
-                    push(k, 0, halo.at[spot], halo_sem.at[spot], near_send.at[k], tm, 1)
+                    push(main.at[spot], halo.at[spot], halo_sem.at[spot], near_send.at[k], tm, 1)
                 )
                 across.append(
-                    push(k, 1, main.at[spot], main_sem.at[spot], far_send.at[k], tm, 1)
+                    push(second, main.at[spot], main_sem.at[spot], far_send.at[k], tm, 1)
                 )
-                kept and stay.append(pltpu.make_async_copy(part(k, 0), main.at[spot], main_sem.at[spot]))
             else:
                 across.append(
-                    push(k, 0, main.at[spot], main_sem.at[spot], near_send.at[k], tm, 0)
+                    push(halo.at[spot], main.at[spot], main_sem.at[spot], near_send.at[k], tm, 0)
                 )
-                kept and stay.append(pltpu.make_async_copy(part(k, 0), halo.at[spot], halo_sem.at[spot]))
-                kept and stay.append(pltpu.make_async_copy(part(k, 1), main.at[spot], main_sem.at[spot]))
-        return ahead, across, stay
+        return ahead, across
 
     for core in range(2):
 
         @pl.when(apa == core)
         def _():
-            ahead, across, stay = sends(core)
-            for copy in ahead + across + stay:
-                copy.start()
+            ahead, across = sends(core)
+            firsts, seconds = own_halves(core)
+            for copy, send in zip(seconds, ahead):
+                copy.wait()
+                send.start()
+            for copy in firsts:
+                copy.wait()
+            for send in across:
+                send.start()
 
     for fetch in fetches[10:]:
         fetch.start()
     for fetch in fetches[:10]:
         fetch.wait()
 
-    build_rows = math.gcd(total.shape[0], 256)
+    build_rows = math.gcd(induction, collection)
     counted = lax.broadcasted_iota(jnp.int32, (build_rows, 2 * CHUNK), 0).astype(jnp.int16)
     one, zero = jnp.bfloat16(1), jnp.bfloat16(0)
+    lane = lax.broadcasted_iota(jnp.int32, (LANES, LANES), 1)
+    row_of = lax.broadcasted_iota(jnp.int32, (LANES, LANES), 0)
 
     def span_of(ref, first, count):
         return ref[pl.ds(pl.multiple_of(first, LANES), count)].reshape(1, count)
@@ -172,15 +195,21 @@
             [span_of(ref, index * CHUNK, CHUNK) for index in (step, pieces + step)], 1
         )
 
-    def make_onehot(step, carry):
-        slot = joined(slots, step)
-        slot = jnp.where(joined(bad, step) == 0, slot, -1)
-        for start in range(0, total.shape[0], build_rows):
-            hit = counted == (slot - start).astype(jnp.int16)
-            onehot[step, start : start + build_rows, :] = jnp.where(hit, one, zero)
+    def plane_rows(slot, start, wires):
+        hits = [
+            jnp.where(counted == (slot - first).astype(jnp.int16), one, zero)
+            for first in range(start, start + wires, build_rows)
+        ]
+        return jnp.concatenate(hits, 0)
+
+    def make_origins(group, carry):
+        first = pl.multiple_of(group * LANES, LANES)
+        delay = span_of(offsets, first, LANES).astype(jnp.float32)
+        delay = jnp.broadcast_to(delay, (LANES, LANES)).T.astype(jnp.int32)
+        origins[pl.ds(first, LANES), :] = (lane - delay) & (LANES - 1)
         return carry
 
-    lax.fori_loop(0, pieces, make_onehot, 0)
+    lax.fori_loop(0, origins.shape[0] // LANES, make_origins, 0)
     total[...] = jnp.zeros_like(total)
 
     spread[...] = jnp.zeros_like(spread)
@@ -197,8 +226,6 @@
         spread[row + count : row + 2 * count, 0:width] = -gain[...] * im / magnitude
     for fetch in fetches[10:]:
         fetch.wait()
-    lane = lax.broadcasted_iota(jnp.int32, (LANES, LANES), 1)
-    row_of = lax.broadcasted_iota(jnp.int32, (LANES, LANES), 0)
     for fine, coarse, count, first, targets, wires in (
         (fine_uv, coarse_uv, 2, 0, (circulant_u, circulant_v), induction),
         (fine_w, coarse_w, 1, 4, (circulant_w,), collection),
@@ -251,27 +278,36 @@
 
     def take(step, carry):
         groups = []
-        for index in (step, pieces + step):
-            pltpu.make_async_copy(main.at[index], main.at[index], main_sem.at[index]).wait()
-            pltpu.make_async_copy(halo.at[index], halo.at[index], halo_sem.at[index]).wait()
+        for half in range(2):
+            index = half * pieces + step
+
+            @pl.when(apa != half)
+            def _():
+                pltpu.make_async_copy(main.at[index], main.at[index], main_sem.at[index]).wait()
+
+            @pl.when(apa * half == 0)
+            def _():
+                pltpu.make_async_copy(halo.at[index], halo.at[index], halo_sem.at[index]).wait()
+
         for index in (step, pieces + step):
             for start in range(0, CHUNK, LANES):
-                delay = span_of(offsets, index * CHUNK + start, LANES).astype(jnp.float32)
-                delay = jnp.broadcast_to(delay, (LANES, LANES)).T.astype(jnp.int32)
-                origin = (lane - delay) & (LANES - 1)
+                origin = origins[
+                    pl.ds(pl.multiple_of(index * CHUNK + start, LANES), LANES), :
+                ]
                 early = halo[index, start : start + LANES, :].astype(jnp.float32)
                 late = main[index, start : start + LANES, :].astype(jnp.float32)
                 early = jnp.take_along_axis(early, origin, axis=1)
                 late = jnp.take_along_axis(late, origin, axis=1)
-                late = jnp.where(lane >= delay, late, early)
+                late = jnp.where(lane >= origin, late, early)
                 groups.append(jnp.concatenate([early, late], 1).astype(jnp.bfloat16))
+        slot = jnp.where(joined(bad, step) == 0, joined(slots, step), -1)
         aligned = jnp.concatenate(groups, 0)
         filtered = jnp.dot(aligned, toeplitz[...], preferred_element_type=jnp.float32).astype(
             jnp.bfloat16
         )
         for plane, (start, wires) in enumerate(zip(starts, sizes)):
             total[start : start + wires, :] += jnp.dot(
-                onehot[step, start : start + wires, :],
+                plane_rows(slot, start, wires),
                 filtered[:, plane * LANES : (plane + 1) * LANES],
                 preferred_element_type=jnp.float32,
             )
@@ -304,23 +340,29 @@
 
         @pl.when(apa == core)
         def _():
-            ahead, across, stay = sends(core, False)
+            ahead, across = sends(core)
             for copy in ahead + across:
                 copy.wait_send()
 
 
-def hand_over(found, out, sems):
-    pieces = sems.shape[0]
+def hand_over(found, out, held, arrive, leave):
+    pieces = arrive.shape[0]
     rows = found.shape[0] // pieces
-    copies = [
-        pltpu.make_async_copy(
-            found.at[pl.ds(k * rows, rows)], out.at[pl.ds(k * rows, rows)], sems.at[k]
-        )
-        for k in range(pieces)
+    spans = [pl.ds(k * rows, rows) for k in range(pieces)]
+    inward = [
+        pltpu.make_async_copy(found.at[span], held.at[span], arrive.at[k])
+        for k, span in enumerate(spans)
     ]
-    for copy in copies:
+    outward = [
+        pltpu.make_async_copy(held.at[span], out.at[span], leave.at[k])
+        for k, span in enumerate(spans)
+    ]
+    for copy in inward:
         copy.start()
-    for copy in copies:
+    for copy, after in zip(inward, outward):
+        copy.wait()
+        after.start()
+    for copy in outward:
         copy.wait()
 
 
@@ -367,7 +409,8 @@
         + [
             pltpu.VMEM((chunks, CHUNK, LANES), jnp.bfloat16),
             pltpu.VMEM((chunks, CHUNK, LANES), jnp.bfloat16),
-            pltpu.VMEM((pieces, channels, 2 * CHUNK), jnp.bfloat16),
+            pltpu.VMEM((pieces, CHUNK, LANES), jnp.bfloat16),
+            pltpu.VMEM((channels, LANES), jnp.int32),
             pltpu.VMEM((channels, LANES), jnp.float32),
             pltpu.VMEM((half_i, padded_i), jnp.bfloat16),
             pltpu.VMEM((half_i, padded_i), jnp.bfloat16),
@@ -383,6 +426,7 @@
             pltpu.SemaphoreType.DMA((pieces,)),
             pltpu.SemaphoreType.DMA((chunks,)),
             pltpu.SemaphoreType.DMA((chunks,)),
+            pltpu.SemaphoreType.DMA((2, pieces)),
             pltpu.SemaphoreType.DMA((len(operands),)),
             pltpu.SemaphoreType.DMA((3,)),
         ],
@@ -395,7 +439,8 @@
         out_shape=jax.ShapeDtypeStruct(found.shape, found.dtype),
         in_specs=[far],
         out_specs=far,
-        scratch_shapes=[pltpu.SemaphoreType.DMA((8,))],
+        scratch_shapes=[pltpu.VMEM(found.shape, found.dtype)]
+        + [pltpu.SemaphoreType.DMA((4,)) for _ in range(2)],
         compiler_params=pltpu.CompilerParams(vmem_limit_bytes=62 * 1024 * 1024),
     )(found)
 

time: 61.2 us -> 20.7 us (0.34)
  Pallas kernels: 61.1 us -> 20.6 us
    pallas_call x1, Pallas kernels: 40.9 us -> 2.09 us  [local(): pl.pallas_call(hand_over, out_shape=jax.ShapeDtypeStruct(found.shape, fou...]
    pallas_call x1, Pallas kernels: 20.2 us -> 18.5 us  [local(): pl.pallas_call(functools.partial(kernel, induction, collection), out_shap...]
where the time goes in v5:
time: 20.7 us; the launch traced here: 20.6 us
  Pallas kernels  20.6 us (100%)
    pallas_call x1, Pallas kernels, local(): pl.pallas_call(functools.partial(kernel, induction, collection), out_shap...  18.5 us
    pallas_call x1, Pallas kernels, local(): pl.pallas_call(hand_over, out_shape=jax.ShapeDtypeStruct(found.shape, fou...  2.09 us

profile of v5, /device:TPU:0, one launch (start us, length us, event | category | flops | bytes accessed | tf_op | source)
XLA Modules:
  0.0 20.6 jit_solution(12887461831157635863)
XLA Ops:
  0.0 18.5 %shard_map.145.found = f32[2560,128]{1,0:T(8,128)} custom-call(bf16[1280,256]{1,0:T(8,128)(2,1)} %waves.1, bf16[3,64]{1,0:T(4,128)(2,1)} %refs_0_.1, s32[2560]{0:T(1024)} %refs_1_.1, s32[2560]{0:T(1024)} %refs_2_.1, s32[2560]{0:T(1024)} %refs_3_.1, f32[2,800]{1,0:T(2,128)} %refs_4_.1, f32[2,800]{1,0:T(2,128)} %refs_5_.1, f32[2,800]{1,0:T(2,128)} %refs_6_.1, ...), custom_call_target="tpu_custom_call" | custom-call | tf_op jit(solution)/shard_map/pallas_call | solution.py:403
  18.5 2.1 %shard_map.146 = f32[2560,128]{1,0:T(8,128)} custom-call(f32[2560,128]{1,0:T(8,128)} %shard_map.145.found), custom_call_target="tpu_custom_call" | custom-call | tf_op jit(solution)/shard_map/pallas_call | solution.py:437

commit v6 on v5

--- a/solution.py
+++ b/solution.py
@@ -55,7 +55,6 @@
         rows_h,
         kernel_rows,
         toeplitz,
-        result,
         next_send,
         near_send,
         far_send,
@@ -63,7 +62,6 @@
         main_sem,
         own_sem,
         fetch_sem,
-        out_sem,
     ) = refs[29:]
     (
         taps,
@@ -315,7 +313,6 @@
 
     lax.fori_loop(0, pieces, take, 0)
 
-    outs = []
     for plane, circulant in enumerate((circulant_u, circulant_v, circulant_w)):
         start, wires = starts[plane], sizes[plane]
         half, spare = wires // 2, rounded_up(wires) - wires
@@ -329,13 +326,8 @@
             jnp.concatenate(stacked, 0),
             preferred_element_type=jnp.float32,
         )
-        result[start : start + half, :] = values[:, 0:LANES]
-        result[start + half : start + wires, :] = values[:, LANES:]
-        span = pl.ds(start, wires)
-        outs.append(pltpu.make_async_copy(result.at[span], out.at[span], out_sem.at[plane]))
-        outs[-1].start()
-    for copy in outs:
-        copy.wait()
+        out[start : start + half, :] = values[:, 0:LANES]
+        out[start + half : start + wires, :] = values[:, LANES:]
     for core in range(2):
 
         @pl.when(apa == core)
@@ -345,24 +337,18 @@
                 copy.wait_send()
 
 
-def hand_over(found, out, held, arrive, leave):
-    pieces = arrive.shape[0]
+def hand_over(found, out, leave):
+    pieces = leave.shape[0]
     rows = found.shape[0] // pieces
-    spans = [pl.ds(k * rows, rows) for k in range(pieces)]
-    inward = [
-        pltpu.make_async_copy(found.at[span], held.at[span], arrive.at[k])
-        for k, span in enumerate(spans)
+    copies = [
+        pltpu.make_async_copy(
+            found.at[pl.ds(k * rows, rows)], out.at[pl.ds(k * rows, rows)], leave.at[k]
+        )
+        for k in range(pieces)
     ]
-    outward = [
-        pltpu.make_async_copy(held.at[span], out.at[span], leave.at[k])
-        for k, span in enumerate(spans)
-    ]
-    for copy in inward:
+    for copy in copies:
         copy.start()
-    for copy, after in zip(inward, outward):
-        copy.wait()
-        after.start()
-    for copy in outward:
+    for copy in copies:
         copy.wait()
 
 
@@ -396,15 +382,16 @@
         collection_real.reshape(1, collection),
         collection_imaginary.reshape(1, collection),
         collection_filter.reshape(1, collection),
-        *phase_tables(induction),
-        *phase_tables(collection),
+        *map(jnp.asarray, phase_tables(induction) + phase_tables(collection)),
     ]
     far = pl.BlockSpec(memory_space=pltpu.HBM)
+    near = pl.BlockSpec(memory_space=pltpu.VMEM)
+    operands = [pltpu.with_memory_space_constraint(operand, pltpu.HBM) for operand in operands]
     found = pl.pallas_call(
         functools.partial(kernel, induction, collection),
-        out_shape=jax.ShapeDtypeStruct((channels, LANES), jnp.float32),
+        out_shape=pltpu.VMEM((channels, LANES), jnp.float32),
         in_specs=[far] * (1 + len(operands)),
-        out_specs=far,
+        out_specs=near,
         scratch_shapes=[pltpu.VMEM(operand.shape, operand.dtype) for operand in operands]
         + [
             pltpu.VMEM((chunks, CHUNK, LANES), jnp.bfloat16),
@@ -420,7 +407,6 @@
             pltpu.VMEM((8, 2 * max(padded_i, padded_c)), jnp.float32),
             pltpu.VMEM((8, LANES), jnp.float32),
             pltpu.VMEM((2 * LANES, 3 * LANES), jnp.bfloat16),
-            pltpu.VMEM((channels, LANES), jnp.float32),
             pltpu.SemaphoreType.DMA((pieces,)),
             pltpu.SemaphoreType.DMA((pieces,)),
             pltpu.SemaphoreType.DMA((pieces,)),
@@ -428,21 +414,18 @@
             pltpu.SemaphoreType.DMA((chunks,)),
             pltpu.SemaphoreType.DMA((2, pieces)),
             pltpu.SemaphoreType.DMA((len(operands),)),
-            pltpu.SemaphoreType.DMA((3,)),
         ],
         compiler_params=pltpu.CompilerParams(
-            collective_id=0, has_side_effects=True, vmem_limit_bytes=62 * 1024 * 1024
+            collective_id=0, has_side_effects=True, vmem_limit_bytes=56 * 1024 * 1024
         ),
-    )(waveforms, *operands)
+    )(pltpu.with_memory_space_constraint(waveforms, pltpu.HBM), *operands)
     return pl.pallas_call(
         hand_over,
         out_shape=jax.ShapeDtypeStruct(found.shape, found.dtype),
-        in_specs=[far],
+        in_specs=[near],
         out_specs=far,
-        scratch_shapes=[pltpu.VMEM(found.shape, found.dtype)]
-        + [pltpu.SemaphoreType.DMA((4,)) for _ in range(2)],
-        compiler_params=pltpu.CompilerParams(vmem_limit_bytes=62 * 1024 * 1024),
-    )(found)
+        scratch_shapes=[pltpu.SemaphoreType.DMA((4,))],
+    )(pltpu.with_memory_space_constraint(found, pltpu.VMEM))
 
 
 def solution(mesh):

time: 20.7 us -> 18.9 us (0.913)
  Pallas kernels: 20.6 us -> 18.7 us
    pallas_call x1, Pallas kernels: 2.09 us -> 1.08 us  [local(): pl.pallas_call(hand_over, out_shape=jax.ShapeDtypeStruct(found.shape, fou...]
    pallas_call x1, Pallas kernels: 18.5 us -> 17.6 us  [local(): pl.pallas_call(functools.partial(kernel, induction, collection), out_shap...]
where the time goes in v6:
time: 18.9 us; the launch traced here: 18.7 us
  Pallas kernels  18.7 us (99%)
    pallas_call x1, Pallas kernels, local(): pl.pallas_call(functools.partial(kernel, induction, collection), out_shap...  17.6 us
    pallas_call x1, Pallas kernels, local(): pl.pallas_call(hand_over, out_shape=jax.ShapeDtypeStruct(found.shape, fou...  1.08 us

profile of v6, /device:TPU:0, one launch (start us, length us, event | category | flops | bytes accessed | tf_op | source)
XLA Modules:
  0.0 18.7 jit_solution(1042767960547189127)
XLA Ops:
  0.0 17.6 %shard_map.145.found = f32[2560,128]{1,0:T(8,128)S(1)} custom-call(bf16[1280,256]{1,0:T(8,128)(2,1)} %waves.1, bf16[3,64]{1,0:T(4,128)(2,1)} %refs_0_.1, s32[2560]{0:T(1024)} %refs_1_.1, s32[2560]{0:T(1024)} %refs_2_.1, s32[2560]{0:T(1024)} %refs_3_.1, f32[2,800]{1,0:T(2,128)} %refs_4_.1, f32[2,800]{1,0:T(2,128)} %refs_5_.1, f32[2,800]{1,0:T(2,128)} %refs_6_.1, ...), custom_call_target="tpu_custom_call" | custom-call | tf_op jit(solution)/shard_map/pallas_call | solution.py:390
  17.6 1.1 %shard_map.146 = f32[2560,128]{1,0:T(8,128)} custom-call(f32[2560,128]{1,0:T(8,128)S(1)} %shard_map.145.found), custom_call_target="tpu_custom_call" | custom-call | tf_op jit(solution)/shard_map/pallas_call | solution.py:422

commit v7 on v6

--- a/solution.py
+++ b/solution.py
@@ -33,6 +33,14 @@
 def halves(values):
     high = values.astype(jnp.bfloat16)
     return high, (values - high.astype(jnp.float32)).astype(jnp.bfloat16)
+
+
+def cut(rows):
+    body = rows - CHUNK
+    return [(first, CHUNK) for first in range(0, body, CHUNK)] + [
+        (body, CHUNK // 2),
+        (body + CHUNK // 2, CHUNK // 2),
+    ]
 
 
 def strided(row):
@@ -55,6 +63,7 @@
         rows_h,
         kernel_rows,
         toeplitz,
+        response_columns,
         next_send,
         near_send,
         far_send,
@@ -83,7 +92,8 @@
     windows = lax.axis_size("tm")
     following = lax.rem(tm + 1, windows)
     previous = lax.rem(tm + windows - 1, windows)
-    pieces = waves.shape[0] // CHUNK
+    held_rows = waves.shape[0]
+    pieces = cut(held_rows)
     sizes = (induction, induction, collection)
     starts = (0, induction, 2 * induction)
 
@@ -107,11 +117,11 @@
     ]
     def own_halves(core):
         copies = ([], [])
-        for k in range(pieces):
-            spot = core * pieces + k
-            targets = (halo.at[spot], main.at[spot]) if core else (main.at[spot], staged.at[k])
+        for k, (first, count) in enumerate(pieces):
+            span, own = pl.ds(first, count), pl.ds(core * held_rows + first, count)
+            targets = (halo.at[own], main.at[own]) if core else (main.at[own], staged.at[span])
             for half in range(2):
-                source = waves.at[pl.ds(k * CHUNK, CHUNK), pl.ds(half * LANES, LANES)]
+                source = waves.at[span, pl.ds(half * LANES, LANES)]
                 copies[half].append(
                     pltpu.make_async_copy(source, targets[half], own_sem.at[half, k])
                 )
@@ -141,23 +151,16 @@
 
     def sends(core):
         ahead, across = [], []
-        for k in range(pieces):
-            spot = core * pieces + k
-            second = main.at[spot] if core else staged.at[k]
-            ahead.append(
-                push(second, halo.at[spot], halo_sem.at[spot], next_send.at[k], following, 0)
-            )
+        for k, (first, count) in enumerate(pieces):
+            span, own = pl.ds(first, count), pl.ds(core * held_rows + first, count)
+            halo_in, main_in = halo_sem.at[core, k], main_sem.at[core, k]
+            second = main.at[own] if core else staged.at[span]
+            ahead.append(push(second, halo.at[own], halo_in, next_send.at[k], following, 0))
             if core == 0:
-                across.append(
-                    push(main.at[spot], halo.at[spot], halo_sem.at[spot], near_send.at[k], tm, 1)
-                )
-                across.append(
-                    push(second, main.at[spot], main_sem.at[spot], far_send.at[k], tm, 1)
-                )
+                across.append(push(main.at[own], halo.at[own], halo_in, near_send.at[k], tm, 1))
+                across.append(push(second, main.at[own], main_in, far_send.at[k], tm, 1))
             else:
-                across.append(
-                    push(halo.at[spot], main.at[spot], main_sem.at[spot], near_send.at[k], tm, 0)
-                )
+                across.append(push(halo.at[own], main.at[own], main_in, near_send.at[k], tm, 0))
         return ahead, across
 
     for core in range(2):
@@ -179,7 +182,7 @@
     for fetch in fetches[:10]:
         fetch.wait()
 
-    build_rows = math.gcd(induction, collection)
+    build_rows = math.gcd(induction // 2, collection // 2)
     counted = lax.broadcasted_iota(jnp.int32, (build_rows, 2 * CHUNK), 0).astype(jnp.int16)
     one, zero = jnp.bfloat16(1), jnp.bfloat16(0)
     lane = lax.broadcasted_iota(jnp.int32, (LANES, LANES), 1)
@@ -188,14 +191,17 @@
     def span_of(ref, first, count):
         return ref[pl.ds(pl.multiple_of(first, LANES), count)].reshape(1, count)
 
-    def joined(ref, step):
-        return jnp.concatenate(
-            [span_of(ref, index * CHUNK, CHUNK) for index in (step, pieces + step)], 1
-        )
+    def slots_of(first, count):
+        def joined(ref):
+            return jnp.concatenate(
+                [span_of(ref, half * held_rows + first, count) for half in range(2)], 1
+            )
+
+        return jnp.where(joined(bad) == 0, joined(slots), -1)
 
     def plane_rows(slot, start, wires):
         hits = [
-            jnp.where(counted == (slot - first).astype(jnp.int16), one, zero)
+            jnp.where(counted[:, : slot.shape[1]] == (slot - first).astype(jnp.int16), one, zero)
             for first in range(start, start + wires, build_rows)
         ]
         return jnp.concatenate(hits, 0)
@@ -274,60 +280,89 @@
             jnp.bfloat16
         )
 
-    def take(step, carry):
+    circulants = (circulant_u, circulant_v, circulant_w)
+    planes = list(zip(circulants, starts, sizes))
+
+    def through(circulant, upper, lower):
+        spare = circulant.shape[1] - 2 * upper.shape[0]
+        stacked = [upper, lower]
+        if spare:
+            stacked.append(jnp.zeros((spare, upper.shape[1]), jnp.bfloat16))
+        return jnp.dot(
+            circulant[0 : upper.shape[0], :],
+            jnp.concatenate(stacked, 0),
+            preferred_element_type=jnp.float32,
+        )
+
+    last = len(pieces) - 1
+    last_slot = slots_of(*pieces[last])
+    for circulant, start, wires in planes:
+        middle = start + wires // 2
+        top = plane_rows(last_slot, start, wires // 2)
+        bottom = plane_rows(last_slot, middle, wires // 2)
+        response_columns[start:middle, :] = through(circulant, top, bottom).astype(jnp.bfloat16)
+        response_columns[middle : start + wires, :] = through(circulant, bottom, top).astype(jnp.bfloat16)
+
+    def filtered_piece(k, first, count):
+        for half in range(2):
+            span = pl.ds(pl.multiple_of(half * held_rows + first, LANES), count)
+
+            @pl.when(apa != half)
+            def _():
+                target = main.at[span]
+                pltpu.make_async_copy(target, target, main_sem.at[half, k]).wait()
+
+            @pl.when(apa * half == 0)
+            def _():
+                target = halo.at[span]
+                pltpu.make_async_copy(target, target, halo_sem.at[half, k]).wait()
+
         groups = []
         for half in range(2):
-            index = half * pieces + step
-
-            @pl.when(apa != half)
-            def _():
-                pltpu.make_async_copy(main.at[index], main.at[index], main_sem.at[index]).wait()
-
-            @pl.when(apa * half == 0)
-            def _():
-                pltpu.make_async_copy(halo.at[index], halo.at[index], halo_sem.at[index]).wait()
-
-        for index in (step, pieces + step):
-            for start in range(0, CHUNK, LANES):
-                origin = origins[
-                    pl.ds(pl.multiple_of(index * CHUNK + start, LANES), LANES), :
-                ]
-                early = halo[index, start : start + LANES, :].astype(jnp.float32)
-                late = main[index, start : start + LANES, :].astype(jnp.float32)
-                early = jnp.take_along_axis(early, origin, axis=1)
-                late = jnp.take_along_axis(late, origin, axis=1)
+            for start in range(0, count, LANES):
+                span = pl.ds(pl.multiple_of(half * held_rows + first + start, LANES), LANES)
+                origin = origins[span, :]
+                early = jnp.take_along_axis(halo[span, :].astype(jnp.float32), origin, axis=1)
+                late = jnp.take_along_axis(main[span, :].astype(jnp.float32), origin, axis=1)
                 late = jnp.where(lane >= origin, late, early)
                 groups.append(jnp.concatenate([early, late], 1).astype(jnp.bfloat16))
-        slot = jnp.where(joined(bad, step) == 0, joined(slots, step), -1)
         aligned = jnp.concatenate(groups, 0)
-        filtered = jnp.dot(aligned, toeplitz[...], preferred_element_type=jnp.float32).astype(
+        return jnp.dot(aligned, toeplitz[...], preferred_element_type=jnp.float32).astype(
             jnp.bfloat16
         )
-        for plane, (start, wires) in enumerate(zip(starts, sizes)):
+
+    def take(k, first, count):
+        filtered = filtered_piece(k, first, count)
+        slot = slots_of(first, count)
+        for plane, (_, start, wires) in enumerate(planes):
             total[start : start + wires, :] += jnp.dot(
                 plane_rows(slot, start, wires),
                 filtered[:, plane * LANES : (plane + 1) * LANES],
                 preferred_element_type=jnp.float32,
             )
+
+    def take_whole(k, carry):
+        take(k, k * CHUNK, CHUNK)
         return carry
 
-    lax.fori_loop(0, pieces, take, 0)
-
-    for plane, circulant in enumerate((circulant_u, circulant_v, circulant_w)):
-        start, wires = starts[plane], sizes[plane]
-        half, spare = wires // 2, rounded_up(wires) - wires
-        top = total[start : start + half, :].astype(jnp.bfloat16)
-        bottom = total[start + half : start + wires, :].astype(jnp.bfloat16)
-        stacked = [jnp.concatenate([top, bottom], 1), jnp.concatenate([bottom, top], 1)]
-        if spare:
-            stacked.append(jnp.zeros((spare, 2 * LANES), jnp.bfloat16))
-        values = jnp.dot(
-            circulant[0:half, :],
-            jnp.concatenate(stacked, 0),
+    lax.fori_loop(0, last - 1, take_whole, 0)
+    take(last - 1, *pieces[last - 1])
+    for circulant, start, wires in planes:
+        middle = start + wires // 2
+        top = total[start:middle, :].astype(jnp.bfloat16)
+        bottom = total[middle : start + wires, :].astype(jnp.bfloat16)
+        values = through(
+            circulant, jnp.concatenate([top, bottom], 1), jnp.concatenate([bottom, top], 1)
+        )
+        out[start:middle, :] = values[:, 0:LANES]
+        out[middle : start + wires, :] = values[:, LANES:]
+    filtered = filtered_piece(last, *pieces[last])
+    for plane, (_, start, wires) in enumerate(planes):
+        out[start : start + wires, :] += jnp.dot(
+            response_columns[start : start + wires, :],
+            filtered[:, plane * LANES : (plane + 1) * LANES],
             preferred_element_type=jnp.float32,
         )
-        out[start : start + half, :] = values[:, 0:LANES]
-        out[start + half : start + wires, :] = values[:, LANES:]
     for core in range(2):
 
         @pl.when(apa == core)
@@ -369,8 +404,7 @@
     induction, collection = induction_real.shape[1], collection_real.shape[0]
     padded_i, padded_c = rounded_up(induction), rounded_up(collection)
     half_i, half_c = rounded_up(induction // 2), rounded_up(collection // 2)
-    chunks = channels // CHUNK
-    pieces = chunks // 2
+    pieces = len(cut(waveforms.shape[0]))
     operands = [
         time_kernel,
         wire_slot,
@@ -394,9 +428,9 @@
         out_specs=near,
         scratch_shapes=[pltpu.VMEM(operand.shape, operand.dtype) for operand in operands]
         + [
-            pltpu.VMEM((chunks, CHUNK, LANES), jnp.bfloat16),
-            pltpu.VMEM((chunks, CHUNK, LANES), jnp.bfloat16),
-            pltpu.VMEM((pieces, CHUNK, LANES), jnp.bfloat16),
+            pltpu.VMEM((channels, LANES), jnp.bfloat16),
+            pltpu.VMEM((channels, LANES), jnp.bfloat16),
+            pltpu.VMEM((channels // 2, LANES), jnp.bfloat16),
             pltpu.VMEM((channels, LANES), jnp.int32),
             pltpu.VMEM((channels, LANES), jnp.float32),
             pltpu.VMEM((half_i, padded_i), jnp.bfloat16),
@@ -407,11 +441,12 @@
             pltpu.VMEM((8, 2 * max(padded_i, padded_c)), jnp.float32),
             pltpu.VMEM((8, LANES), jnp.float32),
             pltpu.VMEM((2 * LANES, 3 * LANES), jnp.bfloat16),
+            pltpu.VMEM((channels, CHUNK), jnp.bfloat16),
             pltpu.SemaphoreType.DMA((pieces,)),
             pltpu.SemaphoreType.DMA((pieces,)),
             pltpu.SemaphoreType.DMA((pieces,)),
-            pltpu.SemaphoreType.DMA((chunks,)),
-            pltpu.SemaphoreType.DMA((chunks,)),
+            pltpu.SemaphoreType.DMA((2, pieces)),
+            pltpu.SemaphoreType.DMA((2, pieces)),
             pltpu.SemaphoreType.DMA((2, pieces)),
             pltpu.SemaphoreType.DMA((len(operands),)),
         ],

time: 18.9 us -> 19.4 us (1.026)
  Pallas kernels: 18.7 us -> 19.2 us
    pallas_call x1, Pallas kernels: 17.6 us -> 18.2 us  [local(): pl.pallas_call(functools.partial(kernel, induction, collection), out_shap...]
where the time goes in v7:
time: 19.4 us; the launch traced here: 19.2 us
  Pallas kernels  19.2 us (99%)
    pallas_call x1, Pallas kernels, local(): pl.pallas_call(functools.partial(kernel, induction, collection), out_shap...  18.2 us
    pallas_call x1, Pallas kernels, local(): pl.pallas_call(hand_over, out_shape=jax.ShapeDtypeStruct(found.shape, fou...  1.08 us

profile of v7, /device:TPU:0, one launch (start us, length us, event | category | flops | bytes accessed | tf_op | source)
XLA Modules:
  0.0 19.2 jit_solution(12455271743494304422)
XLA Ops:
  0.0 18.2 %shard_map.145.found = f32[2560,128]{1,0:T(8,128)S(1)} custom-call(bf16[1280,256]{1,0:T(8,128)(2,1)} %waves.1, bf16[3,64]{1,0:T(4,128)(2,1)} %refs_0_.1, s32[2560]{0:T(1024)} %refs_1_.1, s32[2560]{0:T(1024)} %refs_2_.1, s32[2560]{0:T(1024)} %refs_3_.1, f32[2,800]{1,0:T(2,128)} %refs_4_.1, f32[2,800]{1,0:T(2,128)} %refs_5_.1, f32[2,800]{1,0:T(2,128)} %refs_6_.1, ...), custom_call_target="tpu_custom_call" | custom-call | tf_op jit(solution)/shard_map/pallas_call | solution.py:424
  18.2 1.1 %shard_map.146 = f32[2560,128]{1,0:T(8,128)} custom-call(f32[2560,128]{1,0:T(8,128)S(1)} %shard_map.145.found), custom_call_target="tpu_custom_call" | custom-call | tf_op jit(solution)/shard_map/pallas_call | solution.py:457

commit v8 on v6

--- a/solution.py
+++ b/solution.py
@@ -45,6 +45,7 @@
         halo,
         main,
         staged,
+        onehot,
         origins,
         total,
         circulant_u,
@@ -274,6 +275,14 @@
             jnp.bfloat16
         )
 
+    def make_onehot(step, carry):
+        slot = jnp.where(joined(bad, step) == 0, joined(slots, step), -1)
+        for first in range(0, total.shape[0], build_rows):
+            onehot[step, first : first + build_rows, :] = plane_rows(slot, first, build_rows)
+        return carry
+
+    lax.fori_loop(0, pieces, make_onehot, 0)
+
     def take(step, carry):
         groups = []
         for half in range(2):
@@ -298,14 +307,13 @@
                 late = jnp.take_along_axis(late, origin, axis=1)
                 late = jnp.where(lane >= origin, late, early)
                 groups.append(jnp.concatenate([early, late], 1).astype(jnp.bfloat16))
-        slot = jnp.where(joined(bad, step) == 0, joined(slots, step), -1)
         aligned = jnp.concatenate(groups, 0)
         filtered = jnp.dot(aligned, toeplitz[...], preferred_element_type=jnp.float32).astype(
             jnp.bfloat16
         )
         for plane, (start, wires) in enumerate(zip(starts, sizes)):
             total[start : start + wires, :] += jnp.dot(
-                plane_rows(slot, start, wires),
+                onehot[step, start : start + wires, :],
                 filtered[:, plane * LANES : (plane + 1) * LANES],
                 preferred_element_type=jnp.float32,
             )
@@ -397,6 +405,7 @@
             pltpu.VMEM((chunks, CHUNK, LANES), jnp.bfloat16),
             pltpu.VMEM((chunks, CHUNK, LANES), jnp.bfloat16),
             pltpu.VMEM((pieces, CHUNK, LANES), jnp.bfloat16),
+            pltpu.VMEM((pieces, channels, 2 * CHUNK), jnp.bfloat16),
             pltpu.VMEM((channels, LANES), jnp.int32),
             pltpu.VMEM((channels, LANES), jnp.float32),
             pltpu.VMEM((half_i, padded_i), jnp.bfloat16),

time: 18.9 us -> 18.9 us (level)
  no operation moved by 1% of the time
where the time goes in v8:
time: 18.9 us; the launch traced here: 18.7 us
  Pallas kernels  18.7 us (99%)
    pallas_call x1, Pallas kernels, local(): pl.pallas_call(functools.partial(kernel, induction, collection), out_shap...  17.6 us
    pallas_call x1, Pallas kernels, local(): pl.pallas_call(hand_over, out_shape=jax.ShapeDtypeStruct(found.shape, fou...  1.08 us

profile of v8, /device:TPU:0, one launch (start us, length us, event | category | flops | bytes accessed | tf_op | source)
XLA Modules:
  0.0 18.7 jit_solution(907750745774821846)
XLA Ops:
  0.0 17.6 %shard_map.145.found = f32[2560,128]{1,0:T(8,128)S(1)} custom-call(bf16[1280,256]{1,0:T(8,128)(2,1)} %waves.1, bf16[3,64]{1,0:T(4,128)(2,1)} %refs_0_.1, s32[2560]{0:T(1024)} %refs_1_.1, s32[2560]{0:T(1024)} %refs_2_.1, s32[2560]{0:T(1024)} %refs_3_.1, f32[2,800]{1,0:T(2,128)} %refs_4_.1, f32[2,800]{1,0:T(2,128)} %refs_5_.1, f32[2,800]{1,0:T(2,128)} %refs_6_.1, ...), custom_call_target="tpu_custom_call" | custom-call | tf_op jit(solution)/shard_map/pallas_call | solution.py:398
  17.6 1.1 %shard_map.146 = f32[2560,128]{1,0:T(8,128)} custom-call(f32[2560,128]{1,0:T(8,128)S(1)} %shard_map.145.found), custom_call_target="tpu_custom_call" | custom-call | tf_op jit(solution)/shard_map/pallas_call | solution.py:431

commit v9 on v6

--- a/solution.py
+++ b/solution.py
@@ -40,16 +40,13 @@
 
 
 def kernel(induction, collection, waves, *refs):
-    operands, out, copies = refs[:14], refs[14], refs[15:29]
+    operands, found, copies = refs[:14], refs[14:18], refs[18:32]
+    total, circulant_u, circulant_v, circulant_w = found
     (
         halo,
         main,
         staged,
         origins,
-        total,
-        circulant_u,
-        circulant_v,
-        circulant_w,
         spread,
         folded,
         rows_h,
@@ -62,7 +59,7 @@
         main_sem,
         own_sem,
         fetch_sem,
-    ) = refs[29:]
+    ) = refs[32:]
     (
         taps,
         slots,
@@ -313,11 +310,24 @@
 
     lax.fori_loop(0, pieces, take, 0)
 
+    for core in range(2):
+
+        @pl.when(apa == core)
+        def _():
+            ahead, across = sends(core)
+            for copy in ahead + across:
+                copy.wait_send()
+
+
+def respond(
+    sizes, total, circulant_u, circulant_v, circulant_w, out, result, leave
+):
+    place, copies = 0, []
     for plane, circulant in enumerate((circulant_u, circulant_v, circulant_w)):
-        start, wires = starts[plane], sizes[plane]
-        half, spare = wires // 2, rounded_up(wires) - wires
-        top = total[start : start + half, :].astype(jnp.bfloat16)
-        bottom = total[start + half : start + wires, :].astype(jnp.bfloat16)
+        wires = sizes[plane]
+        half, spare = wires // 2, circulant.shape[1] - wires
+        top = total[place : place + half, :].astype(jnp.bfloat16)
+        bottom = total[place + half : place + wires, :].astype(jnp.bfloat16)
         stacked = [jnp.concatenate([top, bottom], 1), jnp.concatenate([bottom, top], 1)]
         if spare:
             stacked.append(jnp.zeros((spare, 2 * LANES), jnp.bfloat16))
@@ -326,28 +336,12 @@
             jnp.concatenate(stacked, 0),
             preferred_element_type=jnp.float32,
         )
-        out[start : start + half, :] = values[:, 0:LANES]
-        out[start + half : start + wires, :] = values[:, LANES:]
-    for core in range(2):
-
-        @pl.when(apa == core)
-        def _():
-            ahead, across = sends(core)
-            for copy in ahead + across:
-                copy.wait_send()
-
-
-def hand_over(found, out, leave):
-    pieces = leave.shape[0]
-    rows = found.shape[0] // pieces
-    copies = [
-        pltpu.make_async_copy(
-            found.at[pl.ds(k * rows, rows)], out.at[pl.ds(k * rows, rows)], leave.at[k]
-        )
-        for k in range(pieces)
-    ]
-    for copy in copies:
-        copy.start()
+        result[place : place + half, :] = values[:, 0:LANES]
+        result[place + half : place + wires, :] = values[:, LANES:]
+        span = pl.ds(place, wires)
+        copies.append(pltpu.make_async_copy(result.at[span], out.at[span], leave.at[plane]))
+        copies[-1].start()
+        place += wires
     for copy in copies:
         copy.wait()
 
@@ -389,19 +383,20 @@
     operands = [pltpu.with_memory_space_constraint(operand, pltpu.HBM) for operand in operands]
     found = pl.pallas_call(
         functools.partial(kernel, induction, collection),
-        out_shape=pltpu.VMEM((channels, LANES), jnp.float32),
+        out_shape=[
+            pltpu.VMEM((channels, LANES), jnp.float32),
+            pltpu.VMEM((half_i, padded_i), jnp.bfloat16),
+            pltpu.VMEM((half_i, padded_i), jnp.bfloat16),
+            pltpu.VMEM((half_c, padded_c), jnp.bfloat16),
+        ],
         in_specs=[far] * (1 + len(operands)),
-        out_specs=near,
+        out_specs=[near] * 4,
         scratch_shapes=[pltpu.VMEM(operand.shape, operand.dtype) for operand in operands]
         + [
             pltpu.VMEM((chunks, CHUNK, LANES), jnp.bfloat16),
             pltpu.VMEM((chunks, CHUNK, LANES), jnp.bfloat16),
             pltpu.VMEM((pieces, CHUNK, LANES), jnp.bfloat16),
             pltpu.VMEM((channels, LANES), jnp.int32),
-            pltpu.VMEM((channels, LANES), jnp.float32),
-            pltpu.VMEM((half_i, padded_i), jnp.bfloat16),
-            pltpu.VMEM((half_i, padded_i), jnp.bfloat16),
-            pltpu.VMEM((half_c, padded_c), jnp.bfloat16),
             pltpu.VMEM((8, 8 * LANES), jnp.float32),
             pltpu.VMEM((32, 2 * LANES), jnp.float32),
             pltpu.VMEM((8, 2 * max(padded_i, padded_c)), jnp.float32),
@@ -420,12 +415,16 @@
         ),
     )(pltpu.with_memory_space_constraint(waveforms, pltpu.HBM), *operands)
     return pl.pallas_call(
-        hand_over,
-        out_shape=jax.ShapeDtypeStruct(found.shape, found.dtype),
-        in_specs=[near],
+        functools.partial(respond, (induction, induction, collection)),
+        out_shape=jax.ShapeDtypeStruct((channels, LANES), jnp.float32),
+        in_specs=[near] * 4,
         out_specs=far,
-        scratch_shapes=[pltpu.SemaphoreType.DMA((4,))],
-    )(pltpu.with_memory_space_constraint(found, pltpu.VMEM))
+        scratch_shapes=[
+            pltpu.VMEM((channels, LANES), jnp.float32),
+            pltpu.SemaphoreType.DMA((3,)),
+        ],
+        compiler_params=pltpu.CompilerParams(vmem_limit_bytes=32 * 1024 * 1024),
+    )(*[pltpu.with_memory_space_constraint(array, pltpu.VMEM) for array in found])
 
 
 def solution(mesh):

time: 18.9 us -> 18.6 us (0.984)
  Pallas kernels: 18.7 us -> 18.5 us
    pallas_call x1, Pallas kernels: 17.6 us -> 16.8 us  [local(): pl.pallas_call(functools.partial(kernel, induction, collection), out_shap...]
    pallas_call x1, Pallas kernels: 1.08 us -> 1.69 us  [local(): pl.pallas_call(functools.partial(respond, (induction, induction, collecti...]
where the time goes in v9:
time: 18.6 us; the launch traced here: 18.5 us
  Pallas kernels  18.5 us (99%)
    pallas_call x1, Pallas kernels, local(): pl.pallas_call(functools.partial(kernel, induction, collection), out_shap...  16.8 us
    pallas_call x1, Pallas kernels, local(): pl.pallas_call(functools.partial(respond, (induction, induction, collecti...  1.69 us

profile of v9, /device:TPU:0, one launch (start us, length us, event | category | flops | bytes accessed | tf_op | source)
XLA Modules:
  0.0 18.5 jit_solution(9065942439843213116)
XLA Ops:
  0.0 16.8 %shard_map.145 = (f32[2560,128]{1,0:T(8,128)S(1)}, bf16[512,896]{1,0:T(8,128)(2,1)S(1)}, bf16[512,896]{1,0:T(8,128)(2,1)S(1)}, bf16[512,1024]{1,0:T(8,128)(2,1)S(1)}) custom-call(bf16[1280,256]{1,0:T(8,128)(2,1)} %waves.1, bf16[3,64]{1,0:T(4,128)(2,1)} %refs_0_.1, s32[2560]{0:T(1024)} %refs_1_.1, s32[2560]{0:T(1024)} %refs_2_.1, s32[2560]{0:T(1024)} %refs_3_.1, ...), custom_call_target="tpu_custom_call" | custom-call | tf_op jit(solution)/shard_map/pallas_call | solution.py:384
  16.8 1.7 %shard_map.146 = f32[2560,128]{1,0:T(8,128)} custom-call(f32[2560,128]{1,0:T(8,128)S(1)} %get-tuple-element.9.total, bf16[512,896]{1,0:T(8,128)(2,1)S(1)} %get-tuple-element.10.circulant_u, bf16[512,896]{1,0:T(8,128)(2,1)S(1)} %get-tuple-element.11.circulant_v, bf16[512,1024]{1,0:T(8,128)(2,1)S(1)} %get-tuple-element.12.circulant_w), custom_call_target="tpu_custom_call" | custom-call | tf_op jit(solution)/shard_map/pallas_call | solution.py:417
